TPU v7x, 32 devices: a whole 2x2x4 slice. The times are simulated.
32 devices in a mesh: row: 8 (over z, core), col: 4 (over y, x).
Axes of the slice: x: 2, y: 2, z: 4, core: 2. Of those that a mesh axis runs over, the one named last changes fastest.
Arguments:
- moment_one: float32 [1536, 6144], P('row', 'col'), may hold values from -40 to 40
- gradient_one: bfloat16 [1536, 6144], P('row', 'col'), may hold values from -6 to 6
- factor_one: float32 [6144, 384], P(('col', 'row')), may hold values from -6 to 6
- moment_two: float32 [1536, 6144], P('row', 'col'), may hold values from -40 to 40
- gradient_two: bfloat16 [1536, 6144], P('row', 'col'), may hold values from -6 to 6
- factor_two: float32 [1536, 384], P(('row', 'col')), may hold values from -6 to 6
Outputs:
- carried_one: float32 [1536, 6144], P('row', 'col')
- right_next: float32 [6144, 384], P(('col', 'row'))
- carried_two: float32 [1536, 6144], P('row', 'col')
- left_next: float32 [1536, 384], P(('row', 'col'))
All inputs are finite; a program needn't handle non-finite values.
Results may differ from a plain program's by a relative error of at most 0.0003.
Values sent between devices are 32-bit elements; how exact they have to be, the bound alone decides.
No kernel may reach another device: no remote copies, remote signals or barrier semaphores. Data moves between devices by JAX's collectives and lax.ppermute only.
A program may use at most 64 MiB of HBM per device.

v0:
```python
import jax
import jax.numpy as jnp
from jax import lax
from jax.sharding import PartitionSpec as P

momentum_decay = 0.95
epsilon = 1e-06
highest = lax.Precision.HIGHEST


def product_plain(left, right):
    return jnp.dot(left, right, precision=highest, preferred_element_type=jnp.float32)


def product_first(left, right):
    return lax.dot_general(
        left, right, (((0,), (0,)), ((), ())), precision=highest, preferred_element_type=jnp.float32
    )


def product_second(left, right):
    return lax.dot_general(
        left, right, (((1,), (1,)), ((), ())), precision=highest, preferred_element_type=jnp.float32
    )


def solve_basis(gram, panel):
    lower = jnp.linalg.cholesky(gram)
    return lax.linalg.triangular_solve(lower, panel, left_side=False, lower=True, transpose_a=True)


def shards(moment_one, gradient_one, factor_one, moment_two, gradient_two, factor_two):
    buffer_one = moment_one + gradient_one.astype(jnp.float32)
    buffer_two = moment_two + gradient_two.astype(jnp.float32)
    local_rows = buffer_one.shape[0]
    local_cols = buffer_one.shape[1]
    columns = buffer_one
    partial_one = product_plain(columns, lax.all_gather(factor_one, "row", axis=0, tiled=True))
    rows_part = buffer_two
    partial_two = product_first(rows_part, lax.all_gather(factor_two, "col", axis=0, tiled=True))
    panel_one = lax.psum(partial_one, "col")
    gram_one = lax.psum(product_first(panel_one, panel_one), "row")
    basis_one = solve_basis(gram_one, panel_one)
    panel_two = lax.psum(partial_two, "row")
    gram_two = lax.psum(product_first(panel_two, panel_two), "col")
    basis_two = solve_basis(gram_two, panel_two)
    columns = buffer_one
    right_part = lax.psum_scatter(
        product_first(columns, basis_one), "row", scatter_dimension=0, tiled=True
    )
    rows_part = buffer_two
    left_part = lax.psum_scatter(
        product_plain(rows_part, basis_two), "col", scatter_dimension=0, tiled=True
    )
    total_cols = local_cols * lax.axis_size("col")
    total_rows = local_rows * lax.axis_size("row")
    squares_right, squares_left = lax.psum(
        (jnp.sum(right_part * right_part, axis=0), jnp.sum(left_part * left_part, axis=0)),
        ("row", "col"),
    )
    right_next = right_part * lax.rsqrt(squares_right / total_cols + epsilon)
    left_next = left_part * lax.rsqrt(squares_left / total_rows + epsilon)
    correction_one = product_second(
        basis_one, lax.all_gather(right_part, "row", axis=0, tiled=True)
    )
    correction_two = product_second(lax.all_gather(left_part, "col", axis=0, tiled=True), basis_two)
    carried_one = buffer_one - (1.0 - momentum_decay) * correction_one
    carried_two = buffer_two - (1.0 - momentum_decay) * correction_two
    return (carried_one, right_next, carried_two, left_next)


def solution(mesh):
    in_specs = (
        P("row", "col"),
        P("row", "col"),
        P(("col", "row"), None),
        P("row", "col"),
        P("row", "col"),
        P(("row", "col"), None),
    )
    out_specs = (P("row", "col"), P(("col", "row"), None), P("row", "col"), P(("row", "col"), None))
    return jax.shard_map(shards, mesh=mesh, in_specs=in_specs, out_specs=out_specs, check_vma=False)
```

profile of v0, /device:TPU:0, one launch (start us, length us, event | category | flops | bytes accessed | tf_op | source)
XLA Modules:
  0.0 487.0 jit_solution(9445169933805062644)
XLA Ops:
  7.2 0.7 all-gather.3.cloned.1.call-update
  7.9 10.9 %all_gather.14 = f32[192,384]{1,0:T(8,128)S(1)} all-gather(f32[48,384]{1,0:T(8,128)} %param.12), channel_id=1, replica_groups=mesh['row'=8,'col'=4] {'col'}, dimensions={0}, use_global_device_ids=true | all-gather | bytes 368640 | tf_op jit(solution)/shard_map/all_gather | solution.py:40
  18.9 25.1 %all-gather.3.cloned.1.call-done = f32[1536,384]{1,0:T(8,128)} async-done(((f32[192,384]{1,0:T(8,128)}), f32[1536,384]{1,0:T(8,128)}) %all-gather.3.cloned.1.call-update) | async-done | bytes 2359312 | tf_op jit(solution)/shard_map/all_gather | solution.py:38
  44.0 5.1 %fusion.11 = f32[192,384]{1,0:T(8,128)} fusion(f32[1536,384]{1,0:T(8,128)} %all-gather.3.cloned.1.call-done, f32[192,1536]{1,0:T(8,128)} %param.7, bf16[192,1536]{1,0:T(8,128)(2,1)} %param.8), kind=kOutput, calls=%fused_computation.35 | convolution fusion | flops 1359544320 | bytes 4423680 | tf_op jit(solution)/shard_map/dot_general | solution.py:12
  49.2 4.2 fusion.12
  53.4 38.3 %all-reduce.8.cloned.1.call-done = f32[192,384]{1,0:T(8,128)} async-done(((f32[192,384]{1,0:T(8,128)}), f32[192,384]{1,0:T(8,128)}) %all-reduce.8.cloned.1.call-update) | async-done | bytes 294928 | tf_op jit(solution)/shard_map/psum | solution.py:41
  91.7 2.8 fusion.48
  94.6 74.2 %all-reduce.12.cloned.1.call-done = (f32[384,384]{0,1:T(8,128)}, f32[1536,384]{1,0:T(8,128)}) async-done(((f32[384,384]{0,1:T(8,128)}, f32[1536,384]{1,0:T(8,128)}), (f32[384,384]{0,1:T(8,128)}, f32[1536,384]{1,0:T(8,128)})) %all-reduce.12.cloned.1.call-update) | async-done | bytes 2949136 | tf_op jit(solution)/shard_map/psum | solution.py:42
  168.8 7.1 %fusion.49 = f32[384,384]{0,1:T(8,128)} fusion(f32[1536,384]{1,0:T(8,128)} %get-tuple-element.40), kind=kOutput, calls=%fused_computation.111 | convolution fusion | flops 2717908992 | bytes 2949120 | tf_op jit(solution)/shard_map/dot_general | solution.py:16
  176.5 11.7 %cholesky.208 = f32[128,128]{1,0:T(8,128)S(1)} custom-call(f32[128,128]{1,0:T(8,128)S(1)} %cholesky.310), custom_call_target="Cholesky" | custom-call | tf_op jit(solution)/shard_map/jit(cholesky)/cholesky | solution.py:28
  188.3 9.8 %custom-call.24 = f32[1,128,128]{1,2,0:T(8,128)S(1)} custom-call(f32[1,128,128]{2,1,0:T(8,128)S(1)} %get-tuple-element.58), custom_call_target="InvertDiagBlocksLowerTriangular" | custom-call | tf_op jit(solution)/shard_map/jit(cholesky)/cholesky | solution.py:28
  198.4 0.3 convolution_subtract_fusion.3
  198.7 11.7 %cholesky.227 = f32[128,128]{1,0:T(8,128)S(1)} custom-call(f32[128,128]{1,0:T(8,128)S(1)} %cholesky.314), custom_call_target="Cholesky" | custom-call | tf_op jit(solution)/shard_map/jit(cholesky)/cholesky | solution.py:28
  210.5 10.2 %custom-call.25 = f32[1,128,128]{1,2,0:T(8,128)S(1)} custom-call(f32[1,128,128]{2,1,0:T(8,128)S(1)} %get-tuple-element.55), custom_call_target="InvertDiagBlocksLowerTriangular" | custom-call | tf_op jit(solution)/shard_map/jit(cholesky)/cholesky | solution.py:28
  220.9 0.3 convolution_subtract_fusion.7
  221.2 11.7 %cholesky.246 = f32[128,128]{1,0:T(8,128)S(1)} custom-call(f32[128,128]{1,0:T(8,128)S(1)} %convolution_subtract_fusion.7), custom_call_target="Cholesky" | custom-call | tf_op jit(solution)/shard_map/jit(cholesky)/cholesky | solution.py:28
  232.9 0.7 compare_reduce_fusion.3
  233.6 0.6 compare_reduce_fusion.4
  236.3 6.0 %while.2 = (s32[]{:T(128)}, f32[384,384]{1,0:T(8,128)S(1)}, s32[3,2]{0,1:T(2,128)S(1)}, f32[3,128,128]{2,1,0:T(8,128)S(1)}, s32[]{:T(128)}) while((s32[]{:T(128)}, f32[384,384]{1,0:T(8,128)S(1)}, s32[3,2]{0,1:T(2,128)S(1)}, f32[3,128,128]{2,1,0:T(8,128)S(1)}, s32[]{:T(128)}) %tuple.50), condition=%wide.while_cond, body=%wide.while_body.sunk | while | flops 2 | bytes 131181 | solution.py:29
  236.4 0.5 fusion.68
  236.9 1.4 bitcast_dynamic-update-slice_fusion.4
  238.4 0.5 fusion.68
  238.9 1.4 bitcast_dynamic-update-slice_fusion.4
  240.4 0.5 fusion.68
  240.9 1.4 bitcast_dynamic-update-slice_fusion.4
  242.3 29.5 %custom-call.20 = f32[3,128,128]{1,2,0:T(8,128)S(1)} custom-call(f32[3,128,128]{2,1,0:T(8,128)S(1)} %get-tuple-element.12), custom_call_target="InvertDiagBlocksLowerTriangular" | custom-call | tf_op jit(solution)/shard_map/triangular_solve | solution.py:29
  272.6 0.3 convolution_subtract_fusion.5
  273.2 4.1 fusion.10
  277.6 1.4 copy.17
  279.1 11.7 %cholesky.261 = f32[128,128]{1,0:T(8,128)S(1)} custom-call(f32[128,128]{1,0:T(8,128)S(1)} %cholesky.318), custom_call_target="Cholesky" | custom-call | tf_op jit(solution)/shard_map/jit(cholesky)/cholesky | solution.py:28
  290.8 9.8 %custom-call.26 = f32[1,128,128]{1,2,0:T(8,128)S(1)} custom-call(f32[1,128,128]{2,1,0:T(8,128)S(1)} %get-tuple-element.51), custom_call_target="InvertDiagBlocksLowerTriangular" | custom-call | tf_op jit(solution)/shard_map/jit(cholesky)/cholesky | solution.py:28
  301.3 0.6 copy-done.16
  301.9 11.7 %cholesky.280 = f32[128,128]{1,0:T(8,128)S(1)} custom-call(f32[128,128]{1,0:T(8,128)S(1)} %cholesky.322), custom_call_target="Cholesky" | custom-call | tf_op jit(solution)/shard_map/jit(cholesky)/cholesky | solution.py:28
  313.7 10.0 %custom-call.27 = f32[1,128,128]{1,2,0:T(8,128)S(1)} custom-call(f32[1,128,128]{2,1,0:T(8,128)S(1)} %get-tuple-element.48), custom_call_target="InvertDiagBlocksLowerTriangular" | custom-call | tf_op jit(solution)/shard_map/jit(cholesky)/cholesky | solution.py:28
  323.7 1.0 convolution_dynamic-update-slice_fusion
  324.7 1.1 convolution_subtract_fusion.6
  325.9 11.7 %cholesky.299 = f32[128,128]{1,0:T(8,128)S(1)} custom-call(f32[128,128]{1,0:T(8,128)S(1)} %convolution_subtract_fusion.6), custom_call_target="Cholesky" | custom-call | tf_op jit(solution)/shard_map/jit(cholesky)/cholesky | solution.py:28
  337.6 0.6 compare_reduce_fusion.1
  339.6 0.6 compare_reduce_fusion
  340.9 0.9 select_select_fusion
  341.7 8.7 %while.3 = (s32[]{:T(128)}, f32[384,384]{1,0:T(8,128)}, s32[3,2]{0,1:T(2,128)S(1)}, f32[3,128,128]{2,1,0:T(8,128)S(1)}, s32[]{:T(128)}) while((s32[]{:T(128)}, f32[384,384]{1,0:T(8,128)}, s32[3,2]{0,1:T(2,128)S(1)}, f32[3,128,128]{2,1,0:T(8,128)S(1)}, s32[]{:T(128)}) %tuple.71), condition=%wide.while_cond.1, body=%wide.while_body.1.sunk | while | flops 2 | bytes 131181 | solution.py:29
  341.8 0.5 fusion.69
  342.3 2.3 bitcast_dynamic-update-slice_fusion.5
  344.7 0.5 fusion.69
  345.3 2.3 bitcast_dynamic-update-slice_fusion.5
  347.6 0.5 fusion.69
  348.2 2.2 bitcast_dynamic-update-slice_fusion.5
  350.4 30.1 %custom-call.21 = f32[3,128,128]{1,2,0:T(8,128)} custom-call(f32[3,128,128]{2,1,0:T(8,128)S(1)} %get-tuple-element.20), custom_call_target="InvertDiagBlocksLowerTriangular" | custom-call | tf_op jit(solution)/shard_map/triangular_solve | solution.py:29
  380.5 1.7 fusion.6
  382.2 2.3 convolution_subtract_fusion.1
  384.5 0.9 fusion.27
  385.4 3.8 convolution_subtract_fusion
  389.2 0.8 fusion.26
  390.1 0.9 copy-done.6
  391.0 3.2 fusion.2
  394.3 0.7 all-gather.5.cloned.1.call-update
  394.9 23.2 %reduce-scatter.7.cloned.1.call-done = f32[48,384]{1,0:T(8,128)} async-done(((f32[192,384]{1,0:T(8,128)}), f32[48,384]{1,0:T(8,128)}) %reduce-scatter.7.cloned.1.call-update) | async-done | bytes 73744
  418.1 9.3 %all_gather.15 = f32[192,384]{1,0:T(8,128)S(1)} all-gather(f32[48,384]{1,0:T(8,128)} %reduce-scatter.7.cloned.1.call-done), channel_id=1, replica_groups=mesh['row'=8,'col'=4] {'col'}, dimensions={0}, use_global_device_ids=true | all-gather | bytes 368640 | tf_op jit(solution)/shard_map/all_gather | solution.py:66
  427.4 0.9 multiply_reduce_fusion.1
  428.4 4.5 fusion
  432.9 39.5 %all-reduce.2 = (f32[384]{0:T(512)S(1)}, f32[384]{0:T(512)S(1)}) all-reduce(f32[384]{0:T(512)S(1)} %multiply_reduce_fusion, f32[384]{0:T(512)S(1)} %multiply_reduce_fusion.1), channel_id=1, replica_groups=mesh['row'=8,'col'=4] {'row','col'}, use_global_device_ids=true, to_apply=%region_10.12 | all-reduce | flops 768 | bytes 6144 | tf_op jit(solution)/shard_map/psum | solution.py:57
  472.4 0.6 broadcast_multiply_fusion.1
  473.1 0.7 broadcast_multiply_fusion
  473.8 5.9 %fusion.1 = f32[192,1536]{1,0:T(8,128)} fusion(f32[1536,384]{1,0:T(8,128)} %all-gather.5.cloned.1.call-done, f32[192,1536]{1,0:T(8,128)} %param.7, bf16[192,1536]{1,0:T(8,128)(2,1)} %param.8, f32[192,128]{1,0:T(8,128)S(1)} %fusion.31, f32[192,128]{1,0:T(8,128)S(1)} %fusion.32, f32[192,128]{1,0:T(8,128)S(1)} %fusion.24), kind=kOutput, calls=%fused_computation.7 | convolution fusion | flops 1360281600 | bytes 5603328 | tf_op jit(solution)/shard_map/dot_general | solution.py:22
  (86 shorter events, 4.1 us)
Async XLA Ops:
  7.2 36.8 %all-gather.3.cloned.1.call-start = ((), (), s32[]{:S(2)}) async-start(), calls=%async_computation.2 | async-start | bytes 2654208 | tf_op jit(solution)/shard_map/all_gather | solution.py:38
  7.9 83.8 %all-reduce.8.cloned.1.call-start = ((), (), s32[]{:S(2)}) async-start(), calls=%async_computation.3 | async-start | bytes 589824 | tf_op jit(solution)/shard_map/psum | solution.py:41
  18.8 30.3 %copy-start.3 = (f32[192,1536]{1,0:T(8,128)S(1)}, f32[192,1536]{1,0:T(8,128)}, u32[]{:S(2)}) copy-start(f32[192,1536]{1,0:T(8,128)} %param.10) | copy-start | bytes 3538948
  18.8 30.3 %copy-start.7 = (bf16[192,1536]{1,0:T(8,128)(2,1)S(1)}, bf16[192,1536]{1,0:T(8,128)(2,1)}, u32[]{:S(2)}) copy-start(bf16[192,1536]{1,0:T(8,128)(2,1)} %param.11) | copy-start | bytes 1769476
  49.1 119.7 %all-reduce.12.cloned.1.call-start = ((), (), s32[]{:S(2)}) async-start(), calls=%async_computation.8 | async-start | bytes 5898240 | tf_op jit(solution)/shard_map/psum | solution.py:42
  94.5 183.1 %all-reduce.10.cloned.1.call-start = ((), (), s32[]{:S(2)}) async-start(), calls=%async_computation.6 | async-start | bytes 1179648 | tf_op jit(solution)/shard_map/psum | solution.py:45
  168.8 7.4 %copy-start.13 = (f32[384,384]{0,1:T(8,128)S(1)}, f32[384,384]{0,1:T(8,128)}, u32[]{:S(2)}) copy-start(f32[384,384]{0,1:T(8,128)} %get-tuple-element.39) | copy-start | bytes 1769476
  176.0 218.3 %reduce-scatter.5.cloned.1.call-start = ((), (), s32[]{:S(2)}) async-start(), calls=%async_computation.4 | async-start | bytes 2654208 | tf_op jit(solution)/shard_map/reduce_scatter | solution.py:48
  198.7 73.1 %copy-start.10 = (f32[192,384]{1,0:T(8,128)S(1)}, f32[192,384]{1,0:T(8,128)}, u32[]{:S(2)}) copy-start(f32[192,384]{1,0:T(8,128)} %all-reduce.8.cloned.1.call-done) | copy-start | bytes 884740
  236.3 36.9 %copy-start.5 = (f32[192,1536]{1,0:T(8,128)S(1)}, f32[192,1536]{1,0:T(8,128)}, u32[]{:S(2)}) copy-start(f32[192,1536]{1,0:T(8,128)} %param.7) | copy-start | bytes 3538948
  236.3 36.9 %copy-start.9 = (bf16[192,1536]{1,0:T(8,128)(2,1)S(1)}, bf16[192,1536]{1,0:T(8,128)(2,1)}, u32[]{:S(2)}) copy-start(bf16[192,1536]{1,0:T(8,128)(2,1)} %param.8) | copy-start | bytes 1769476
  277.4 140.8 %reduce-scatter.7.cloned.1.call-start = ((), (), s32[]{:S(2)}) async-start(), calls=%async_computation.7 | async-start | bytes 368640
  277.6 1.4 copy-start.12
  279.1 21.9 %copy-start.14 = (f32[384,384]{1,0:T(8,128)}, f32[384,384]{1,0:T(8,128)S(1)}, u32[]{:S(2)}) copy-start(f32[384,384]{1,0:T(8,128)S(1)} %fusion.8) | copy-start | bytes 1769476
  301.3 0.7 copy-start.16
  301.9 78.6 %copy-start = (f32[1536,384]{1,0:T(8,128)S(1)}, f32[1536,384]{1,0:T(8,128)}, u32[]{:S(2)}) copy-start(f32[1536,384]{1,0:T(8,128)} %get-tuple-element.40) | copy-start | bytes 7077892
  382.2 2.3 copy-start.17
  385.4 4.7 copy-start.1
  385.4 5.6 %copy-start.8 = (bf16[192,1536]{1,0:T(8,128)(2,1)S(1)}, bf16[192,1536]{1,0:T(8,128)(2,1)}, u32[]{:S(2)}) copy-start(bf16[192,1536]{1,0:T(8,128)(2,1)} %param.11) | copy-start | bytes 1769476
  389.2 1.8 copy-start.4
  390.1 0.9 copy-start.6
  394.2 34.2 %copy-start.2 = (f32[1536,128]{0,1:T(8,128)S(1)}, f32[1536,128]{0,1:T(8,128)}, u32[]{:S(2)}) copy-start(f32[1536,128]{0,1:T(8,128)} %copy-done.1) | copy-start | bytes 2359300
  394.2 79.6 %all-gather.5.cloned.1.call-start = ((), (), s32[]{:S(2)}) async-start(), calls=%async_computation.5 | async-start | bytes 2654208 | tf_op jit(solution)/shard_map/all_gather | solution.py:64
  428.4 4.5 copy-start.11
  428.4 44.1 %copy-start.15 = (f32[48,384]{1,0:T(8,128)S(1)}, f32[48,384]{1,0:T(8,128)}, u32[]{:S(2)}) copy-start(f32[48,384]{1,0:T(8,128)} %reduce-scatter.7.cloned.1.call-done) | copy-start | bytes 221188
Sparse Core Ops, SparseCore 0:
  9.6 34.3 all-gather.2
  49.2 42.4 all-reduce.7
  94.9 73.8 all-reduce.11
  176.1 46.2 all-reduce.9
  277.5 36.1 reduce-scatter.4
  394.3 23.7 reduce-scatter.6
  419.9 31.6 all-gather.4
where the time goes:
time: 495 us; the launch traced here: 487 us
  other arithmetic  176 us (36%)
  waiting for transfers between devices  162 us (33%)
  blocking collectives  59.7 us (12%)
  matrix products  51.4 us (10%)
  between operations  19 us (4%)
  local copies, waits for them, and re-layouts  17.9 us (4%)
    another operation x20, other arithmetic, solve_basis(): lower = jnp.linalg.cholesky(gram)  113 us
    psum x1, waiting for transfers between devices, shards(): gram_one = lax.psum(product_first(panel_one, panel_one), 'row')  74.2 us
    another operation x5, other arithmetic, solve_basis(): lax.linalg.triangular_solve(lower, panel, left_side=False, lower=True, tr...  60.5 us
    psum x1, blocking collectives, shards(): lax.psum((jnp.sum(right_part * right_part, axis=0), jnp.sum(left_part * l...  39.5 us
    psum x1, waiting for transfers between devices, shards(): panel_one = lax.psum(partial_one, 'col')  38.3 us
    all_gather x1, waiting for transfers between devices, shards(): lax.all_gather(factor_one, 'row', axis=0, tiled=True)  25.1 us
    unnamed x8, waiting for transfers between devices  24.6 us
    dot_general x4, matrix products, product_first(): lax.dot_general(left, right, (((0,), (0,)), ((), ())), precision=highest,...  18.2 us
  transfers between devices with their start and end apart: 7, of which 4 were waited for; matrix products, arithmetic and copies ran while one was open for 46% of the time, Pallas kernels for 0%

commit v1 on v0

v1 whole, which is shorter than its diff:
```python
import functools

import jax
import jax.numpy as jnp
from jax import lax
from jax.experimental import pallas as pl
from jax.experimental.pallas import tpu as pltpu
from jax.sharding import PartitionSpec as P

momentum_decay = 0.95
epsilon = 1e-06
highest = lax.Precision.HIGHEST
tile = 128
lead = 3
chunks = 3
free = pl.CostEstimate(flops=1, bytes_accessed=1, transcendentals=0)


def product(left, right, over_left, over_right, precision=highest):
    return lax.dot_general(
        left,
        right,
        (((over_left,), (over_right,)), ((), ())),
        precision=precision,
        preferred_element_type=jnp.float32,
    )


def split(x):
    high = x.astype(jnp.bfloat16)
    return high, (x - high.astype(jnp.float32)).astype(jnp.bfloat16)


def product_split(left, right, over_left, over_right):
    (a, b), (c, d) = split(left), split(right)
    one = lambda x, y: product(x, y, over_left, over_right, None)
    return one(a, d) + one(b, c) + one(a, c)


class Flow:
    def __init__(self):
        z, core = row_place()
        self.place = jnp.stack((lax.axis_index("col"), z, core)).astype(jnp.int32)
        self.last = ()

    def __call__(self, kernel, outs, *args, scratch=()):
        last = len(self.last)
        whole = pl.BlockSpec(memory_space=pltpu.VMEM)

        def body(*refs):
            kernel(*refs[last:])

        results = pl.pallas_call(
            body,
            out_shape=[jax.ShapeDtypeStruct(shape, jnp.float32) for shape in outs],
            in_specs=[pl.BlockSpec(memory_space=pl.ANY)] * last
            + [pl.BlockSpec(memory_space=pltpu.SMEM)]
            + [whole] * len(args),
            out_specs=[whole] * len(outs),
            scratch_shapes=[pltpu.VMEM(shape, jnp.float32) for shape in scratch],
            compiler_params=pltpu.CompilerParams(vmem_limit_bytes=24 * 2**20),
            cost_estimate=free,
            name=getattr(kernel, "func", kernel).__name__,
        )(*self.last, self.place, *args)
        self.last = (results[-1],)
        return results


class Task:
    def __init__(self, steps):
        self.steps, self.result = steps, None

    def step(self, times=1):
        for _ in range(times):
            if self.steps is not None:
                try:
                    next(self.steps)
                except StopIteration as end:
                    self.steps, self.result = None, end.value
        return self

    def finish(self):
        while self.steps is not None:
            self.step()
        return self.result


def many(start, size):
    return pl.ds(pl.multiple_of(start, tile), size)


def eliminate(blocks):
    lane = lax.broadcasted_iota(jnp.int32, (8, tile), 1)
    sub = lax.broadcasted_iota(jnp.int32, (8, tile), 0)
    count = tile // 8
    work = [[block[8 * i : 8 * i + 8, :] for i in range(count)] for block in blocks]

    def spread(rows, j):
        return {i: jnp.broadcast_to(rows[i][:, j : j + 1], (8, tile)) for i in range(j // 8, count)}

    ahead = [{j: spread(rows, j) for j in range(lead)} for rows in work]
    for j in range(tile):
        t, s = divmod(j, 8)
        for rows, columns in zip(work, ahead):
            if j + lead < tile:
                columns[j + lead] = spread(rows, j + lead)
            column = columns.pop(j)
            inverse = 1.0 / column[t][s : s + 1, :]
            pivot = jnp.where(lane[:1] == j, 1.0, rows[t][s : s + 1, :]) * inverse
            pivot = jnp.broadcast_to(pivot, (8, tile))
            for later, values in columns.items():
                u, v = divmod(later, 8)
                weight = jnp.broadcast_to(column[u][v : v + 1, :] * inverse, (8, tile))
                for i in values:
                    values[i] = values[i] - column[i] * weight
            for i in range(t, count):
                below, hit = column[i], lane == j
                if i == t:
                    if s == 7:
                        continue
                    below = jnp.where(sub > s, below, 0.0)
                    hit = hit & (sub > s)
                rows[i] = jnp.where(hit, 0.0, rows[i]) - below * pivot
    outs = []
    for rows in work:
        out = []
        for i in range(count):
            row = sub + 8 * i
            diagonal = jnp.sum(jnp.where(lane == row, rows[i], 0.0), axis=1, keepdims=True)
            scale = lax.rsqrt(diagonal)
            scale = scale * (1.5 - 0.5 * diagonal * scale * scale)
            out.append(jnp.where(lane < row, rows[i], jnp.where(lane == row, 1.0, 0.0)) * scale)
        outs.append(jnp.concatenate(out, axis=0))
    return outs


def inverse_blocks(grams, outs):
    blocks = grams[0].shape[0] // tile
    at = lambda i: slice(tile * i, tile * i + tile)
    every = range(len(grams))
    rest = [{(i, j): g[at(i), at(j)] for i in range(blocks) for j in range(i + 1)} for g in grams]
    diagonal = [{} for _ in every]
    lower = [{} for _ in every]
    for b in range(blocks):
        found = eliminate([rest[m][b, b] for m in every])
        for m in every:
            diagonal[m][b] = found[m]
            for i in range(b + 1, blocks):
                lower[m][i, b] = product(rest[m][i, b], found[m], 1, 1)
            for i in range(b + 1, blocks):
                for j in range(b + 1, i + 1):
                    rest[m][i, j] = rest[m][i, j] - product(lower[m][i, b], lower[m][j, b], 1, 1)
    for m in every:
        inverse = {}
        for i in range(blocks):
            inverse[i, i] = diagonal[m][i]
            for j in range(i):
                total = product(lower[m][i, j], inverse[j, j], 1, 0)
                for k in range(j + 1, i):
                    total = total + product(lower[m][i, k], inverse[k, j], 1, 0)
                inverse[i, j] = -product(diagonal[m][i], total, 1, 0)
        for i in range(blocks):
            for j in range(blocks):
                outs[m][at(i), at(j)] = inverse[i, j] if j <= i else jnp.zeros((tile, tile), jnp.float32)


def inverse_kernel(place, *refs):
    *stripes, mine, other, out_one, out_two, gram_one, gram_two = refs
    col, core = place[0], place[2]
    rows = stripes[0].shape[0]
    for bits, stripe in enumerate(stripes):
        gram_one[pl.ds(pl.multiple_of((col ^ bits) * rows, 8), rows), :] = stripe[...]
    half = mine.shape[0]
    gram_two[pl.ds(pl.multiple_of(core * half, 8), half), :] = mine[...]
    gram_two[pl.ds(pl.multiple_of((1 - core) * half, 8), half), :] = other[...]
    inverse_blocks((gram_one, gram_two), (out_one, out_two))


def rows_of(refs):
    return jnp.concatenate([r[...] for r in refs], axis=0)


def half_buffer(moment, gradient, core, half):
    at = many(core * half, half)
    return moment[:, at] + gradient[:, at].astype(jnp.float32)


def give_kernel(place, moment, gradient, *refs):
    *parts, out = refs
    buffer = half_buffer(moment, gradient, 1 - place[2], out.shape[0])
    out[...] = product_split(buffer, rows_of(parts), 0, 0)


def keep_kernel(count, place, moment, gradient, came, *refs):
    parts, outs = refs[:count], refs[count:]
    half = came.shape[0]
    rows = half // len(outs)
    value = product_split(half_buffer(moment, gradient, place[2], half), rows_of(parts), 0, 0) + came[...]
    for i, out in enumerate(outs):
        out[...] = value[i * rows : (i + 1) * rows]


def add_kernel(place, *refs):
    count = len(refs) // 3
    for i in range(count):
        refs[2 * count + i][...] = refs[2 * i][...] + refs[2 * i + 1][...]


def total_kernel(place, *refs):
    *parts, out = refs
    total = parts[0][...]
    for part in parts[1:]:
        total = total + part[...]
    out[...] = total


def pick_kernel(low, high, place, x, moved, out):
    ends = (place[1] == low) | (place[1] == high)
    out[...] = jnp.where(ends, moved[...], x[...])


def order_kernel(place, mine, other, out):
    first = place[2] == 0
    a, b = mine[...], other[...]
    out[...] = jnp.concatenate((jnp.where(first, a, b), jnp.where(first, b, a)), axis=0)


def stack_kernel(place, own, *refs):
    *moved, out = refs
    count = len(moved) // 2
    up, down = moved[:count], moved[count:]
    rows = own.shape[0]
    out[:rows, :] = own[...]
    for s in range(1, count + 1):
        out[s * rows : (s + 1) * rows, :] = up[count - s][...] + down[s - 1][...]


def first_panel(line, place, moment, gradient, mine, other, low, high):
    width = moment.shape[1] // line
    rows = width // 2
    first = place[2] == 0
    total = None
    for s in range(line):
        at = many(lax.rem(place[1] + s, line) * width, width)
        buffer = moment[:, at] + gradient[:, at].astype(jnp.float32)
        a, b = mine[s * rows : (s + 1) * rows, :], other[s * rows : (s + 1) * rows, :]
        factor = jnp.concatenate((jnp.where(first, a, b), jnp.where(first, b, a)), axis=0)
        term = product_split(buffer, factor, 1, 0)
        total = term if total is None else total + term
    half = low.shape[0]
    low[...] = total[:half]
    high[...] = total[half:]


def stripe_kernel(place, low, high, keep, give, gram):
    panel = rows_of((low, high))
    gram[...] = product(panel, panel, 0, 0)
    half = keep.shape[0]
    stripe = gram[pl.ds(pl.multiple_of(place[0] * 2 * half, 8), 2 * half), :]
    first = place[2] == 0
    keep[...] = jnp.where(first, stripe[:half], stripe[half:])
    give[...] = jnp.where(first, stripe[half:], stripe[:half])


def gram_kernel(place, *refs):
    *parts, keep, give = refs
    panel = rows_of(parts)
    gram = product(panel, panel, 0, 0)
    half = keep.shape[0]
    first = place[2] == 0
    keep[...] = jnp.where(first, gram[:half], gram[half:])
    give[...] = jnp.where(first, gram[half:], gram[:half])


def second_product(count, place, moment, gradient, *refs):
    mine, other, (low, high) = refs[:count], refs[count : 2 * count], refs[2 * count :]
    total = None
    for core, parts in ((place[2], mine), (1 - place[2], other)):
        panel = rows_of(parts)
        at = many(core * panel.shape[0], panel.shape[0])
        term = product_split(moment[:, at] + gradient[:, at].astype(jnp.float32), panel, 1, 0)
        total = term if total is None else total + term
    half = low.shape[0]
    low[...] = total[:half]
    high[...] = total[half:]


def right_kernel(count, place, *refs):
    mine, other, (inverse, out, squares) = refs[:count], refs[count : 2 * count], refs[2 * count :]
    total = None
    for core, parts in ((place[2], mine), (1 - place[2], other)):
        value = product_split(rows_of(parts), inverse[...], 1, 1)
        out[pl.ds(pl.multiple_of(core * value.shape[0], 8), value.shape[0]), :] = value
        term = jnp.sum(value * value, axis=0, keepdims=True)
        total = term if total is None else total + term
    squares[...] = total


def left_kernel(place, low, high, inverse, out, weight, squares):
    value = product_split(rows_of((low, high)), inverse[...], 1, 1)
    out[...] = value
    weight[...] = product_split(value, inverse[...], 1, 0)
    squares[...] = jnp.sum(value * value, axis=0, keepdims=True)


def carry(moment, gradient, at, weight, panel, out):
    change = product_split(weight, panel, 1, 1)
    out[:, at] = moment[:, at] + gradient[:, at].astype(jnp.float32) - (1.0 - momentum_decay) * change


def carry_one_kernel(place, moment, gradient, low, high, inverse, right, out):
    weight = product_split(rows_of((low, high)), inverse[...], 1, 1)
    step = right.shape[0] // 2
    for i in range(2):
        at = pl.ds(i * step, step)
        carry(moment, gradient, at, weight, right[at, :], out)


def carry_two_kernel(count, place, moment, gradient, *refs):
    mine, other, (weight, out) = refs[:count], refs[count : 2 * count], refs[2 * count :]
    for core, parts in ((place[2], mine), (1 - place[2], other)):
        panel = rows_of(parts)
        at = many(core * panel.shape[0], panel.shape[0])
        carry(moment, gradient, at, weight[...], panel, out)


def line_size():
    return lax.axis_size("row") // 2


def row_place():
    me = lax.axis_index("row")
    return me // 2, me % 2


def swap_core(x):
    return lax.ppermute(x, "row", [(i, i ^ 1) for i in range(lax.axis_size("row"))])


def move_line(x, pairs):
    return lax.ppermute(x, "row", [(2 * a + k, 2 * b + k) for a, b in pairs for k in range(2)])


def turn_line(x, step):
    line = line_size()
    return move_line(x, [(z, (z + step) % line) for z in range(line)])


def swap_col(x, bits):
    return lax.ppermute(x, "col", [(i, i ^ bits) for i in range(lax.axis_size("col"))])


def gather_line(flow, x):
    line = line_size()
    up, down = [x], [x]
    for s in range(1, line):
        up.append(move_line(up[-1], [(z, z + 1) for z in range(s - 1, line - 1)]))
        down.append(move_line(down[-1], [(z, z - 1) for z in range(1, line - s + 1)]))
    mine = flow(stack_kernel, [(line * x.shape[0], x.shape[1])], *up, *down[1:])[0]
    return mine, swap_core(mine)


def sum_line(flow, x):
    line = line_size()
    half = line // 2
    for h in range(half - 1):
        moved = move_line(x, [(h, h + 1), (line - 1 - h, line - 2 - h)])
        yield
        x = flow(add_kernel, [x.shape], x, moved)[0]
    moved = move_line(x, [(half - 1, half), (half, half - 1)])
    yield
    x = flow(add_kernel, [x.shape], x, moved)[0]
    for h in range(half - 2, -1, -1):
        moved = move_line(x, [(h + 1, h), (line - 2 - h, line - 1 - h)])
        yield
        x = flow(functools.partial(pick_kernel, h, line - 1 - h), [x.shape], x, moved)[0]
    return x, swap_core(x)


def col_bits():
    return [1 << b for b in range((lax.axis_size("col") - 1).bit_length())]


def sum_col(flow, low, high):
    bits = col_bits()
    for up, down in zip(bits, bits[::-1]):
        moved = swap_col(low, up), swap_col(high, down)
        yield
        low, high = flow(add_kernel, [low.shape, high.shape], low, moved[0], high, moved[1])
    return low, high


def gather_col(x):
    me = lax.axis_index("col")
    rows = x.shape[0]
    out = jnp.zeros((lax.axis_size("col") * rows,) + x.shape[1:], x.dtype)
    for bits in range(lax.axis_size("col")):
        piece = swap_col(x, bits) if bits else x
        out = lax.dynamic_update_slice(out, piece, ((me ^ bits) * rows, 0))
    return out


def rows_at(x, start, rows):
    return lax.dynamic_slice_in_dim(x, start, rows, 0)


def gram_stripes(flow, low, high):
    cols = lax.axis_size("col")
    size = low.shape[1]
    shape = (size // (2 * cols), size)
    keep, give = flow(stripe_kernel, [shape, shape], low, high, scratch=[(size, size)])
    moved = swap_core(give)
    yield
    part = flow(add_kernel, [shape], keep, moved)[0]
    moved = [turn_line(part, s) for s in range(1, line_size())]
    yield
    part = flow(total_kernel, [shape], part, *moved)[0]
    moved = swap_core(part)
    yield
    stripe = flow(order_kernel, [(2 * shape[0], size)], part, moved)[0]
    return [stripe] + [swap_col(stripe, bits) for bits in range(1, cols)]


def gram_halves(flow, parts):
    size = parts[0].shape[1]
    shape = (size // 2, size)
    part, give = flow(gram_kernel, [shape, shape], *parts)
    moved = swap_core(give)
    yield
    part = flow(add_kernel, [shape], part, moved)[0]
    for bits in col_bits():
        moved = swap_col(part, bits)
        yield
        part = flow(add_kernel, [shape], part, moved)[0]
    return [part, swap_core(part)]


def sum_squares(flow, right, left):
    moved = [swap_col(right, b) for b in range(1, lax.axis_size("col"))]
    came = swap_core(left)
    yield
    left = flow(add_kernel, [left.shape], left, came)[0]
    turned = [turn_line(left, s) for s in range(1, line_size())]
    yield
    return functools.reduce(jnp.add, moved, right), functools.reduce(jnp.add, turned, left)


def shards(moment_one, gradient_one, factor_one, moment_two, gradient_two, factor_two):
    flow = Flow()
    col = lax.axis_index("col")
    cols = lax.axis_size("col")
    line = line_size()
    one, two = (moment_one, gradient_one), (moment_two, gradient_two)
    local_rows, local_cols = moment_one.shape
    rank = factor_one.shape[1]
    total_cols = local_cols * cols
    total_rows = local_rows * lax.axis_size("row")
    half = (local_cols // 2, rank)
    chunk = (half[0] // chunks, rank)
    low_high = [(local_rows // 2, rank)] * 2
    block = (local_rows, rank)
    square = (rank, rank)

    def transposed(buffer, *parts):
        came = swap_core(flow(give_kernel, [half], *buffer, *parts)[0])
        yield
        kernel = functools.partial(keep_kernel, len(parts))
        values = flow(kernel, [chunk] * chunks, *buffer, came, *parts)
        return [Task(sum_line(flow, value)).step() for value in values]

    panel_two = Task(transposed(two, gather_col(factor_two))).step().finish()

    factor = gather_line(flow, factor_one)
    panel_one = flow(functools.partial(first_panel, line), low_high, *one, *factor)
    panel_one = Task(sum_col(flow, *panel_one)).step()
    panel_two[0].step()
    panel_one.step()
    panel_two[1].step()
    panel_one = panel_one.finish()

    right = Task(transposed(one, *panel_one)).step()
    gram_one = Task(gram_stripes(flow, *panel_one)).step()
    right = right.finish()
    gram_one.step()
    panel_two[2].step()
    panel_two[0].step()
    panel_two[1].step()
    gram_one.step()
    right[0].step()
    panel_two[2].step()
    gram_one = gram_one.finish()
    panel_two[0].finish()
    right[1].step()
    panel_two[1].finish()
    right[2].step()
    panel_two[2].finish()

    panel_two = [part for task in panel_two for part in task.result]
    panel_two = panel_two[::2] + panel_two[1::2]
    gram_two = Task(gram_halves(flow, panel_two[:chunks])).step(2)
    left = flow(functools.partial(second_product, chunks), low_high, *two, *panel_two)
    left = Task(sum_col(flow, *left)).step()
    right[0].step()
    gram_two.step()
    left.step()
    right[1].step()
    gram_two = gram_two.finish()
    left = left.finish()
    right[2].step()

    inverse_one, inverse_two = flow(
        inverse_kernel, [square, square], *gram_one, *gram_two, scratch=[square, square]
    )
    right = [part for task in right for part in task.finish()]
    right = right[::2] + right[1::2]

    left_sum, weight_two, squares_left = flow(left_kernel, [block, block, (1, rank)], *left, inverse_two)
    kernel = functools.partial(right_kernel, chunks)
    right_sum, squares_right = flow(kernel, [(local_cols, rank), (1, rank)], *right, inverse_one)
    squares = Task(sum_squares(flow, squares_right, squares_left)).step(2)
    kernel = functools.partial(carry_two_kernel, chunks)
    carried_two = flow(kernel, [moment_two.shape], *two, *panel_two, weight_two)[0]
    carried_one = flow(carry_one_kernel, [moment_one.shape], *one, *panel_one, inverse_one, right_sum)[0]
    squares_right, squares_left = squares.finish()

    right_rows = local_cols // (2 * line)
    right_part = rows_at(right_sum, lax.axis_index("row") * right_rows, right_rows)
    left_rows = local_rows // cols
    left_part = rows_at(left_sum, col * left_rows, left_rows)
    right_next = right_part * lax.rsqrt(squares_right / total_cols + epsilon)
    left_next = left_part * lax.rsqrt(squares_left / total_rows + epsilon)
    return (carried_one, right_next, carried_two, left_next)


def solution(mesh):
    in_specs = (
        P("row", "col"),
        P("row", "col"),
        P(("col", "row"), None),
        P("row", "col"),
        P("row", "col"),
        P(("row", "col"), None),
    )
    out_specs = (P("row", "col"), P(("col", "row"), None), P("row", "col"), P(("row", "col"), None))
    return jax.shard_map(shards, mesh=mesh, in_specs=in_specs, out_specs=out_specs, check_vma=False)
```

time: 495 us -> 237 us (0.48); the launches traced: 487 us -> 236 us
  other arithmetic: 176 us -> 3.09 us
  starting transfers between devices: 0.67 us -> 76.5 us
  waiting for transfers between devices: 162 us -> 87.2 us
  blocking collectives: 59.7 us -> 0 us
  Pallas kernels: 0 us -> 57.4 us
  matrix products: 51.4 us -> 0 us
  between operations: 19 us -> 1.54 us
  local copies, waits for them, and re-layouts: 17.9 us -> 10.7 us
    another operation x25 -> x1, other arithmetic: 173 us -> 0.08 us  [__init__(): self.place = jnp.stack((lax.axis_index('col'), z, core)).astype(jnp.int32)]
    psum x3 -> x0, waiting for transfers between devices: 113 us -> none  [the longest x1 74.2 us: shards(): gram_one = lax.psum(product_first(panel_one, panel_one), 'row')]
    ppermute x0 -> x63, waiting for transfers between devices: none -> 87.2 us  [the longest x30 61.9 us: move_line(): lax.ppermute(x, 'row', [(2 * a + k, 2 * b + k) for a, b in pairs for k in...]
    ppermute x0 -> x63, starting transfers between devices: none -> 76.5 us  [the longest x30 56.4 us: move_line(): lax.ppermute(x, 'row', [(2 * a + k, 2 * b + k) for a, b in pairs for k in...]
    pallas_call x0 -> x43, Pallas kernels: none -> 57.4 us  [__call__(): pl.pallas_call(body, out_shape=[jax.ShapeDtypeStruct(shape, jnp.float32)...]
    psum x1 -> x0, blocking collectives: 39.5 us -> none  [shards(): lax.psum((jnp.sum(right_part * right_part, axis=0), jnp.sum(left_part * l...]
    dot_general x8 -> x0, matrix products: 36.9 us -> none  [the longest x4 18.2 us: product_first(): lax.dot_general(left, right, (((0,), (0,)), ((), ())), precision=highest,...]
    all_gather x2 -> x0, waiting for transfers between devices: 25.1 us -> none  [the longest x1 25.1 us: shards(): lax.all_gather(factor_one, 'row', axis=0, tiled=True)]
  transfers between devices with their start and end apart: 7 -> 63, of which waited for: 4 -> 20; matrix products, arithmetic and copies ran while one was open for 46% -> 1% of each run, Pallas kernels for 0% -> 21%
where the time goes in v1:
time: 237 us; the launch traced here: 236 us
  waiting for transfers between devices  87.2 us (37%)
  starting transfers between devices  76.5 us (32%)
  Pallas kernels  57.4 us (24%)
  local copies, waits for them, and re-layouts  10.7 us (5%)
  other arithmetic  3.09 us (1%)
    ppermute x30, waiting for transfers between devices, move_line(): lax.ppermute(x, 'row', [(2 * a + k, 2 * b + k) for a, b in pairs for k in...  61.9 us
    pallas_call x43, Pallas kernels, __call__(): pl.pallas_call(body, out_shape=[jax.ShapeDtypeStruct(shape, jnp.float32)...  57.4 us
    ppermute x30, starting transfers between devices, move_line(): lax.ppermute(x, 'row', [(2 * a + k, 2 * b + k) for a, b in pairs for k in...  56.4 us
    ppermute x19, waiting for transfers between devices, swap_col(): lax.ppermute(x, 'col', [(i, i ^ bits) for i in range(lax.axis_size('col'))])  25.3 us
    ppermute x19, starting transfers between devices, swap_col(): lax.ppermute(x, 'col', [(i, i ^ bits) for i in range(lax.axis_size('col'))])  17.3 us
    unnamed x54, local copies, waits for them, and re-layouts  9.71 us
  transfers between devices with their start and end apart: 63, of which 20 were waited for; matrix products, arithmetic and copies ran while one was open for 1% of the time, Pallas kernels for 21%

profile of v1, /device:TPU:0, one launch (start us, length us, event | category | flops | bytes accessed | tf_op | source)
XLA Modules:
  0.0 236.5 jit_solution(12673915672276720329)
XLA Ops:
  0.6 3.0 %collective-permute-start = (f32[48,384]{1,0:T(8,128)}, f32[48,384]{1,0:T(8,128)S(1)}, u32[]{:S(2)}, u32[]{:S(2)}) collective-permute-start(f32[48,384]{1,0:T(8,128)} %param.11), channel_id=1, source_target_pairs={{0,1},{1,0},{2,3},{3,2},{4,5},{5,4},{6,7},{7,6},{8,9},{9,8},{10,11... | collective-permute-start | bytes 221192 | tf_op jit(solution)/shard_map/ppermute | solution.py:350
  3.6 1.5 collective-permute-start.1
  6.5 1.7 collective-permute-done.1
  8.2 2.4 %collective-permute-done.2 = f32[48,384]{1,0:T(8,128)S(1)} collective-permute-done((f32[48,384]{1,0:T(8,128)}, f32[48,384]{1,0:T(8,128)S(1)}, u32[]{:S(2)}, u32[]{:S(2)}) %collective-permute-start.2) | collective-permute-done | bytes 73760 | tf_op jit(solution)/shard_map/ppermute | solution.py:350
  10.7 1.3 copy-done
  11.9 1.4 give_kernel.2.refs_0_
  13.4 3.5 %collective-permute-start.4 = (f32[192,384]{1,0:T(8,128)S(1)}, f32[192,384]{1,0:T(8,128)S(1)}, u32[]{:S(2)}, u32[]{:S(2)}) collective-permute-start(f32[192,384]{1,0:T(8,128)S(1)} %copy-done.25), channel_id=1, source_target_pairs={{0,8},{4,12},{8,16},{12,20},{16,24},{20,28},{1,9},{5,13},{9,17},{1... | collective-permute-start | bytes 884744 | tf_op jit(solution)/shard_map/ppermute | solution.py:341
  16.9 1.3 collective-permute-start.7
  18.2 5.6 %collective-permute-done.4.refs_3_ = f32[192,384]{1,0:T(8,128)S(1)} collective-permute-done((f32[192,384]{1,0:T(8,128)S(1)}, f32[192,384]{1,0:T(8,128)S(1)}, u32[]{:S(2)}, u32[]{:S(2)}) %collective-permute-start.4) | collective-permute-done | bytes 294944 | tf_op jit(solution)/shard_map/ppermute | solution.py:341
  24.4 3.5 %collective-permute-done.7.refs_6_ = f32[192,384]{1,0:T(8,128)S(1)} collective-permute-done((f32[192,384]{1,0:T(8,128)S(1)}, f32[192,384]{1,0:T(8,128)S(1)}, u32[]{:S(2)}, u32[]{:S(2)}) %collective-permute-start.7) | collective-permute-done | bytes 294944 | tf_op jit(solution)/shard_map/ppermute | solution.py:341
  27.9 1.3 collective-permute-start.8
  29.9 8.4 %collective-permute-done.8.refs_7_ = f32[192,384]{1,0:T(8,128)S(1)} collective-permute-done((f32[192,384]{1,0:T(8,128)S(1)}, f32[192,384]{1,0:T(8,128)S(1)}, u32[]{:S(2)}, u32[]{:S(2)}) %collective-permute-start.8) | collective-permute-done | bytes 294944 | tf_op jit(solution)/shard_map/ppermute | solution.py:341
  38.2 1.3 collective-permute-start.9
  39.5 1.4 keep_kernel.2
  40.9 6.7 %collective-permute-done.9.refs_8_ = f32[192,384]{1,0:T(8,128)S(1)} collective-permute-done((f32[192,384]{1,0:T(8,128)S(1)}, f32[192,384]{1,0:T(8,128)S(1)}, u32[]{:S(2)}, u32[]{:S(2)}) %collective-permute-start.9) | collective-permute-done | bytes 294944 | tf_op jit(solution)/shard_map/ppermute | solution.py:341
  48.4 1.5 collective-permute-start.11
  49.9 1.3 collective-permute-start.14
  51.3 1.9 first_panel.1
  54.3 5.0 %collective-permute-done.11.refs_3_ = f32[256,384]{1,0:T(8,128)S(1)} collective-permute-done((f32[256,384]{1,0:T(8,128)S(1)}, f32[256,384]{1,0:T(8,128)S(1)}, u32[]{:S(2)}, u32[]{:S(2)}) %collective-permute-start.11) | collective-permute-done | bytes 393248 | tf_op jit(solution)/shard_map/ppermute | solution.py:341
  61.0 1.2 collective-permute-start.16
  62.2 5.2 %collective-permute-done.14.refs_3_ = f32[256,384]{1,0:T(8,128)S(1)} collective-permute-done((f32[256,384]{1,0:T(8,128)S(1)}, f32[256,384]{1,0:T(8,128)S(1)}, u32[]{:S(2)}, u32[]{:S(2)}) %collective-permute-start.14) | collective-permute-done | bytes 393248 | tf_op jit(solution)/shard_map/ppermute | solution.py:341
  68.6 1.4 give_kernel.3.refs_0_
  70.1 4.4 %collective-permute-start.19 = (f32[256,384]{1,0:T(8,128)S(1)}, f32[256,384]{1,0:T(8,128)S(1)}, u32[]{:S(2)}, u32[]{:S(2)}) collective-permute-start(f32[256,384]{1,0:T(8,128)S(1)} %get-tuple-element.33.refs_0_.refs_2_), channel_id=1, source_target_pairs={{0,8},{4,12},{24,16},{28,20},{1,9},{5,13},{25,17},{29,21},{2,10},{... | collective-permute-start | bytes 1179656 | tf_op jit(solution)/shard_map/ppermute | solution.py:341
  75.9 1.4 stripe_kernel.1
  77.6 1.4 keep_kernel.3
  79.0 5.6 %collective-permute-start.25 = (f32[256,384]{1,0:T(8,128)S(1)}, f32[256,384]{1,0:T(8,128)S(1)}, u32[]{:S(2)}, u32[]{:S(2)}) collective-permute-start(f32[256,384]{1,0:T(8,128)S(1)} %get-tuple-element.45.refs_2_), channel_id=1, source_target_pairs={{0,8},{4,12},{24,16},{28,20},{1,9},{5,13},{25,17},{29,21},{2,10},{... | collective-permute-start | bytes 1179656 | tf_op jit(solution)/shard_map/ppermute | solution.py:341
  86.4 2.1 collective-permute-start.22
  88.6 1.5 collective-permute-start.23
  90.1 2.8 %collective-permute-start.24 = (f32[48,384]{1,0:T(8,128)S(1)}, f32[48,384]{1,0:T(8,128)S(1)}, u32[]{:S(2)}, u32[]{:S(2)}) collective-permute-start(f32[48,384]{1,0:T(8,128)S(1)} %add_kernel.25.refs_0_.refs_2_), channel_id=1, source_target_pairs={{0,24},{4,28},{8,0},{12,4},{16,8},{20,12},{24,16},{28,20},{1,25},{... | collective-permute-start | bytes 221192 | tf_op jit(solution)/shard_map/ppermute | solution.py:341
  94.1 3.1 %collective-permute-done.22.refs_3_ = f32[48,384]{1,0:T(8,128)S(1)} collective-permute-done((f32[48,384]{1,0:T(8,128)S(1)}, f32[48,384]{1,0:T(8,128)S(1)}, u32[]{:S(2)}, u32[]{:S(2)}) %collective-permute-start.22) | collective-permute-done | bytes 73760 | tf_op jit(solution)/shard_map/ppermute | solution.py:341
  97.2 11.5 %collective-permute-done.23.refs_4_ = f32[48,384]{1,0:T(8,128)S(1)} collective-permute-done((f32[48,384]{1,0:T(8,128)S(1)}, f32[48,384]{1,0:T(8,128)S(1)}, u32[]{:S(2)}, u32[]{:S(2)}) %collective-permute-start.23) | collective-permute-done | bytes 73760 | tf_op jit(solution)/shard_map/ppermute | solution.py:341
  109.4 1.3 collective-permute-start.28
  110.7 4.6 %collective-permute-start.29 = (f32[256,384]{1,0:T(8,128)S(1)}, f32[256,384]{1,0:T(8,128)S(1)}, u32[]{:S(2)}, u32[]{:S(2)}) collective-permute-start(f32[256,384]{1,0:T(8,128)S(1)} %get-tuple-element.46.refs_2_), channel_id=1, source_target_pairs={{0,8},{4,12},{24,16},{28,20},{1,9},{5,13},{25,17},{29,21},{2,10},{... | collective-permute-start | bytes 1179656 | tf_op jit(solution)/shard_map/ppermute | solution.py:341
  115.3 1.3 collective-permute-start.30
  117.2 4.6 %collective-permute-start.31 = (f32[256,384]{1,0:T(8,128)S(1)}, f32[256,384]{1,0:T(8,128)S(1)}, u32[]{:S(2)}, u32[]{:S(2)}) collective-permute-start(f32[256,384]{1,0:T(8,128)S(1)} %get-tuple-element.43.refs_0_.refs_2_), channel_id=1, source_target_pairs={{0,8},{4,12},{24,16},{28,20},{1,9},{5,13},{25,17},{29,21},{2,10},{... | collective-permute-start | bytes 1179656 | tf_op jit(solution)/shard_map/ppermute | solution.py:341
  122.4 1.3 collective-permute-start.32
  125.5 6.1 %collective-permute-done.30.refs_3_ = f32[256,384]{1,0:T(8,128)S(1)} collective-permute-done((f32[256,384]{1,0:T(8,128)S(1)}, f32[256,384]{1,0:T(8,128)S(1)}, u32[]{:S(2)}, u32[]{:S(2)}) %collective-permute-start.30) | collective-permute-done | bytes 393248 | tf_op jit(solution)/shard_map/ppermute | solution.py:341
  133.0 6.6 %collective-permute-done.32.refs_3_ = f32[256,384]{1,0:T(8,128)S(1)} collective-permute-done((f32[256,384]{1,0:T(8,128)S(1)}, f32[256,384]{1,0:T(8,128)S(1)}, u32[]{:S(2)}, u32[]{:S(2)}) %collective-permute-start.32) | collective-permute-done | bytes 393248 | tf_op jit(solution)/shard_map/ppermute | solution.py:341
  140.2 2.6 %gram_kernel.1 = (f32[192,384]{1,0:T(8,128)S(1)}, f32[192,384]{1,0:T(8,128)S(1)}) custom-call(f32[256,384]{1,0:T(8,128)S(1)} %pick_kernel.8.refs_0_.refs_4_.refs_6_, s32[3]{0:T(128)S(1)} %pad_add_fusion.refs_0_.refs_1_, f32[256,384]{1,0:T(8,128)S(1)} %pick_kernel.6.refs_0_.refs_2_.refs_4_, f32[256,384]{1,0:T(8,128)S(1)} %pick_kernel.7.refs_0_.refs_3_.refs_5_, ...), custom_call_target="tpu_custom_call" | custom-call | flops 1 | bytes 1 | tf_op jit(solution)/shard_map/gram_kernel/pallas_call | solution.py:53
  147.3 1.7 second_product.1
  149.0 1.6 collective-permute-start.39
  151.6 3.5 %collective-permute-done.38.refs_3_ = f32[192,384]{1,0:T(8,128)S(1)} collective-permute-done((f32[192,384]{1,0:T(8,128)S(1)}, f32[192,384]{1,0:T(8,128)S(1)}, u32[]{:S(2)}, u32[]{:S(2)}) %collective-permute-start.38) | collective-permute-done | bytes 294944 | tf_op jit(solution)/shard_map/ppermute | solution.py:350
  156.3 1.1 collective-permute-done.39.refs_3_
  159.2 1.4 collective-permute-start.46
  161.2 3.4 %collective-permute-done.42.refs_3_ = f32[192,384]{1,0:T(8,128)S(1)} collective-permute-done((f32[192,384]{1,0:T(8,128)S(1)}, f32[192,384]{1,0:T(8,128)S(1)}, u32[]{:S(2)}, u32[]{:S(2)}) %collective-permute-start.42) | collective-permute-done | bytes 294944 | tf_op jit(solution)/shard_map/ppermute | solution.py:350
  164.6 1.3 collective-permute-start.50
  166.5 1.3 collective-permute-start.51
  169.0 1.5 collective-permute-start.52
  171.1 6.2 %collective-permute-done.47.refs_4_ = f32[96,384]{1,0:T(8,128)S(1)} collective-permute-done((f32[96,384]{1,0:T(8,128)S(1)}, f32[96,384]{1,0:T(8,128)S(1)}, u32[]{:S(2)}, u32[]{:S(2)}) %collective-permute-start.47) | collective-permute-done | bytes 147488 | tf_op jit(solution)/shard_map/ppermute | solution.py:350
  177.3 6.0 %collective-permute-done.48.refs_5_ = f32[96,384]{1,0:T(8,128)S(1)} collective-permute-done((f32[96,384]{1,0:T(8,128)S(1)}, f32[96,384]{1,0:T(8,128)S(1)}, u32[]{:S(2)}, u32[]{:S(2)}) %collective-permute-start.48) | collective-permute-done | bytes 147488 | tf_op jit(solution)/shard_map/ppermute | solution.py:350
  183.3 15.7 %inverse_kernel.1 = (f32[384,384]{1,0:T(8,128)S(1)}, f32[384,384]{1,0:T(8,128)S(1)}) custom-call(f32[256,384]{1,0:T(8,128)S(1)} %add_kernel.40.refs_0_.refs_2_, s32[3]{0:T(128)S(1)} %pad_add_fusion.refs_0_.refs_1_, f32[96,384]{1,0:T(8,128)S(1)} %order_kernel.1.refs_0_.refs_2_, f32[96,384]{1,0:T(8,128)S(1)} %collective-permute-done.46.refs_3_, ...), custom_call_target="tpu_custom_call" | custom-call | flops 1 | bytes 1 | tf_op jit(solution)/shard_map/inverse_kernel/pallas_call | solution.py:53
  201.6 1.5 left_kernel.1
  204.4 2.9 %right_kernel.1 = (f32[1536,384]{1,0:T(8,128)S(1)}, f32[1,384]{1,0:T(1,128)S(1)}) custom-call(f32[1,384]{1,0:T(1,128)S(1)} %get-tuple-element.56.refs_0_.refs_2_, s32[3]{0:T(128)S(1)} %pad_add_fusion.refs_0_.refs_1_, f32[256,384]{1,0:T(8,128)S(1)} %pick_kernel.9.refs_0_.refs_2_, f32[256,384]{1,0:T(8,128)S(1)} %pick_kernel.10.refs_0_.refs_3_, ...), custom_call_target="tpu_custom_call" | custom-call | flops 1 | bytes 1 | tf_op jit(solution)/shard_map/right_kernel/pallas_call | solution.py:53
  207.3 1.4 copy-done.11
  209.2 3.5 %collective-permute-start.60 = (f32[1,384]{1,0:T(1,128)S(1)}, f32[1,384]{1,0:T(1,128)S(1)}, u32[]{:S(2)}, u32[]{:S(2)}) collective-permute-start(f32[1,384]{1,0:T(1,128)S(1)} %add_kernel.41.refs_0_), channel_id=1, source_target_pairs={{0,8},{4,12},{8,16},{12,20},{16,24},{20,28},{24,0},{28,4},{1,9},{5... | collective-permute-start | bytes 4616 | tf_op jit(solution)/shard_map/ppermute | solution.py:341
  213.6 2.8 %collective-permute-start.62 = (f32[1,384]{1,0:T(1,128)S(1)}, f32[1,384]{1,0:T(1,128)}, u32[]{:S(2)}, u32[]{:S(2)}) collective-permute-start(f32[1,384]{1,0:T(1,128)S(1)} %add_kernel.41.refs_0_), channel_id=1, source_target_pairs={{0,24},{4,28},{8,0},{12,4},{16,8},{20,12},{24,16},{28,20},{1,25},{... | collective-permute-start | bytes 4616 | tf_op jit(solution)/shard_map/ppermute | solution.py:341
  217.0 1.3 collective-permute-start.58
  218.3 1.1 copy-done.5
  221.3 1.0 copy-done.22
  223.3 2.9 %carry_two_kernel.1.refs_0_ = f32[192,1536]{1,0:T(8,128)} custom-call(f32[1,384]{1,0:T(1,128)S(1)} %add_kernel.41.refs_0_, s32[3]{0:T(128)S(1)} %pad_add_fusion.refs_0_.refs_1_, f32[192,1536]{1,0:T(8,128)S(1)} %copy-done.1, bf16[192,1536]{1,0:T(8,128)(2,1)S(1)} %copy-done.5, f32[256,384]{1,0:T(8,128)S(1)} %pick_kernel.6.refs_0_.refs_2_.refs_4_, ...), custom_call_target="tpu_custom_call" | custom-call | flops 1 | bytes 1 | tf_op jit(solution)/shard_map/carry_two_kernel/pallas_call | solution.py:53
  226.3 1.3 copy-done.8
  227.5 3.7 %carry_one_kernel.1 = f32[192,1536]{1,0:T(8,128)} custom-call(f32[192,1536]{1,0:T(8,128)S(1)} %copy-done.8, s32[3]{0:T(128)S(1)} %pad_add_fusion.refs_0_.refs_1_, f32[192,1536]{1,0:T(8,128)S(1)} %copy-done.2, bf16[192,1536]{1,0:T(8,128)(2,1)S(1)} %copy-done.7, f32[96,384]{1,0:T(8,128)S(1)} %copy-done.16, f32[96,384]{1,0:T(8,128)S(1)} %copy-done.10, ...), custom_call_target="tpu_custom_call" | custom-call | flops 1 | bytes 1 | tf_op jit(solution)/shard_map/carry_one_kernel/pallas_call | solution.py:53
  231.2 1.7 collective-permute-start.59
  233.6 1.5 dynamic-slice_multiply_fusion.1
  (169 shorter events, 39.7 us)
Async XLA Ops:
  0.6 10.0 %copy-start.3 = (bf16[192,1536]{1,0:T(8,128)(2,1)S(1)}, bf16[192,1536]{1,0:T(8,128)(2,1)}, u32[]{:S(2)}) copy-start(bf16[192,1536]{1,0:T(8,128)(2,1)} %refs_3_.12) | copy-start | bytes 1769476
  0.6 5.8 %collective-permute-start = (f32[48,384]{1,0:T(8,128)}, f32[48,384]{1,0:T(8,128)S(1)}, u32[]{:S(2)}, u32[]{:S(2)}) collective-permute-start(f32[48,384]{1,0:T(8,128)} %param.11), channel_id=1, source_target_pairs={{0,1},{1,0},{2,3},{3,2},{4,5},{5,4},{6,7},{7,6},{8,9},{9,8},{10,11... | collective-permute-start | bytes 221192 | tf_op jit(solution)/shard_map/ppermute | solution.py:350
  3.6 4.6 %collective-permute-start.1 = (f32[48,384]{1,0:T(8,128)}, f32[48,384]{1,0:T(8,128)S(1)}, u32[]{:S(2)}, u32[]{:S(2)}) collective-permute-start(f32[48,384]{1,0:T(8,128)} %param.11), channel_id=1, source_target_pairs={{0,2},{1,3},{2,0},{3,1},{4,6},{5,7},{6,4},{7,5},{8,10},{9,11},{10,... | collective-permute-start | bytes 221192 | tf_op jit(solution)/shard_map/ppermute | solution.py:350
  5.2 5.5 %collective-permute-start.2 = (f32[48,384]{1,0:T(8,128)}, f32[48,384]{1,0:T(8,128)S(1)}, u32[]{:S(2)}, u32[]{:S(2)}) collective-permute-start(f32[48,384]{1,0:T(8,128)} %param.11), channel_id=1, source_target_pairs={{0,3},{1,2},{2,1},{3,0},{4,7},{5,6},{6,5},{7,4},{8,11},{9,10},{10,... | collective-permute-start | bytes 221192 | tf_op jit(solution)/shard_map/ppermute | solution.py:350
  13.3 26.2 %collective-permute-start.3 = (f32[768,384]{1,0:T(8,128)S(1)}, f32[768,384]{1,0:T(8,128)S(1)}, u32[]{:S(2)}, u32[]{:S(2)}) collective-permute-start(f32[768,384]{1,0:T(8,128)S(1)} %give_kernel.2.refs_0_), channel_id=1, source_target_pairs={{0,4},{4,0},{8,12},{12,8},{16,20},{20,16},{24,28},{28,24},{1,5},{5... | collective-permute-start | bytes 3538952 | tf_op jit(solution)/shard_map/ppermute | solution.py:337
  13.4 10.4 %collective-permute-start.4 = (f32[192,384]{1,0:T(8,128)S(1)}, f32[192,384]{1,0:T(8,128)S(1)}, u32[]{:S(2)}, u32[]{:S(2)}) collective-permute-start(f32[192,384]{1,0:T(8,128)S(1)} %copy-done.25), channel_id=1, source_target_pairs={{0,8},{4,12},{8,16},{12,20},{16,24},{20,28},{1,9},{5,13},{9,17},{1... | collective-permute-start | bytes 884744 | tf_op jit(solution)/shard_map/ppermute | solution.py:341
  16.9 11.0 %collective-permute-start.7 = (f32[192,384]{1,0:T(8,128)S(1)}, f32[192,384]{1,0:T(8,128)S(1)}, u32[]{:S(2)}, u32[]{:S(2)}) collective-permute-start(f32[192,384]{1,0:T(8,128)S(1)} %copy-done.25), channel_id=1, source_target_pairs={{8,0},{12,4},{16,8},{20,12},{24,16},{28,20},{9,1},{13,5},{17,9},{2... | collective-permute-start | bytes 884744 | tf_op jit(solution)/shard_map/ppermute | solution.py:341
  23.8 5.4 %collective-permute-start.5 = (f32[192,384]{1,0:T(8,128)S(1)}, f32[192,384]{1,0:T(8,128)S(1)}, u32[]{:S(2)}, u32[]{:S(2)}) collective-permute-start(f32[192,384]{1,0:T(8,128)S(1)} %collective-permute-done.4.refs_3_), channel_id=1, source_target_pairs={{8,16},{12,20},{16,24},{20,28},{9,17},{13,21},{17,25},{21,29},{10,... | collective-permute-start | bytes 884744 | tf_op jit(solution)/shard_map/ppermute | solution.py:341
  27.9 10.3 %collective-permute-start.8 = (f32[192,384]{1,0:T(8,128)S(1)}, f32[192,384]{1,0:T(8,128)S(1)}, u32[]{:S(2)}, u32[]{:S(2)}) collective-permute-start(f32[192,384]{1,0:T(8,128)S(1)} %collective-permute-done.7.refs_6_), channel_id=1, source_target_pairs={{8,0},{12,4},{16,8},{20,12},{9,1},{13,5},{17,9},{21,13},{10,2},{14... | collective-permute-start | bytes 884744 | tf_op jit(solution)/shard_map/ppermute | solution.py:341
  29.2 11.7 %collective-permute-start.6 = (f32[192,384]{1,0:T(8,128)S(1)}, f32[192,384]{1,0:T(8,128)S(1)}, u32[]{:S(2)}, u32[]{:S(2)}) collective-permute-start(f32[192,384]{1,0:T(8,128)S(1)} %collective-permute-done.5.refs_4_), channel_id=1, source_target_pairs={{16,24},{20,28},{17,25},{21,29},{18,26},{22,30},{19,27},{23,31}} | collective-permute-start | bytes 884744 | tf_op jit(solution)/shard_map/ppermute | solution.py:341
  38.2 9.4 %collective-permute-start.9 = (f32[192,384]{1,0:T(8,128)S(1)}, f32[192,384]{1,0:T(8,128)S(1)}, u32[]{:S(2)}, u32[]{:S(2)}) collective-permute-start(f32[192,384]{1,0:T(8,128)S(1)} %collective-permute-done.8.refs_7_), channel_id=1, source_target_pairs={{8,0},{12,4},{9,1},{13,5},{10,2},{14,6},{11,3},{15,7}} | collective-permute-start | bytes 884744 | tf_op jit(solution)/shard_map/ppermute | solution.py:341
  48.3 2.9 %collective-permute-start.10 = (f32[768,384]{1,0:T(8,128)S(1)}, f32[768,384]{1,0:T(8,128)S(1)}, u32[]{:S(2)}, u32[]{:S(2)}) collective-permute-start(f32[768,384]{1,0:T(8,128)S(1)} %stack_kernel.1.refs_0_.refs_4_), channel_id=1, source_target_pairs={{0,4},{4,0},{8,12},{12,8},{16,20},{20,16},{24,28},{28,24},{1,5},{5... | collective-permute-start | bytes 3538952 | tf_op jit(solution)/shard_map/ppermute | solution.py:337
  48.4 10.9 %collective-permute-start.11 = (f32[256,384]{1,0:T(8,128)S(1)}, f32[256,384]{1,0:T(8,128)S(1)}, u32[]{:S(2)}, u32[]{:S(2)}) collective-permute-start(f32[256,384]{1,0:T(8,128)S(1)} %get-tuple-element.35.refs_2_), channel_id=1, source_target_pairs={{0,8},{4,12},{24,16},{28,20},{1,9},{5,13},{25,17},{29,21},{2,10},{... | collective-permute-start | bytes 1179656 | tf_op jit(solution)/shard_map/ppermute | solution.py:341
  49.9 17.5 %collective-permute-start.14 = (f32[256,384]{1,0:T(8,128)S(1)}, f32[256,384]{1,0:T(8,128)S(1)}, u32[]{:S(2)}, u32[]{:S(2)}) collective-permute-start(f32[256,384]{1,0:T(8,128)S(1)} %get-tuple-element.38.refs_2_), channel_id=1, source_target_pairs={{0,8},{4,12},{24,16},{28,20},{1,9},{5,13},{25,17},{29,21},{2,10},{... | collective-permute-start | bytes 1179656 | tf_op jit(solution)/shard_map/ppermute | solution.py:341
  53.2 6.7 %collective-permute-start.12 = (f32[96,384]{1,0:T(8,128)S(1)}, f32[96,384]{1,0:T(8,128)S(1)}, u32[]{:S(2)}, u32[]{:S(2)}) collective-permute-start(f32[96,384]{1,0:T(8,128)S(1)} %get-tuple-element.36.refs_2_), channel_id=1, source_target_pairs={{0,1},{1,0},{2,3},{3,2},{4,5},{5,4},{6,7},{7,6},{8,9},{9,8},{10,11... | collective-permute-start | bytes 442376 | tf_op jit(solution)/shard_map/ppermute | solution.py:350
  53.8 6.1 %collective-permute-start.13 = (f32[96,384]{1,0:T(8,128)S(1)}, f32[96,384]{1,0:T(8,128)S(1)}, u32[]{:S(2)}, u32[]{:S(2)}) collective-permute-start(f32[96,384]{1,0:T(8,128)S(1)} %get-tuple-element.34.refs_0_.refs_4_), channel_id=1, source_target_pairs={{0,2},{1,3},{2,0},{3,1},{4,6},{5,7},{6,4},{7,5},{8,10},{9,11},{10,... | collective-permute-start | bytes 442376 | tf_op jit(solution)/shard_map/ppermute | solution.py:350
  60.5 7.5 %collective-permute-start.15 = (f32[96,384]{1,0:T(8,128)S(1)}, f32[96,384]{1,0:T(8,128)S(1)}, u32[]{:S(2)}, u32[]{:S(2)}) collective-permute-start(f32[96,384]{1,0:T(8,128)S(1)} %get-tuple-element.39.refs_2_), channel_id=1, source_target_pairs={{0,2},{1,3},{2,0},{3,1},{4,6},{5,7},{6,4},{7,5},{8,10},{9,11},{10,... | collective-permute-start | bytes 442376 | tf_op jit(solution)/shard_map/ppermute | solution.py:350
  61.0 7.0 %collective-permute-start.16 = (f32[96,384]{1,0:T(8,128)S(1)}, f32[96,384]{1,0:T(8,128)S(1)}, u32[]{:S(2)}, u32[]{:S(2)}) collective-permute-start(f32[96,384]{1,0:T(8,128)S(1)} %get-tuple-element.37.refs_0_.refs_4_), channel_id=1, source_target_pairs={{0,1},{1,0},{2,3},{3,2},{4,5},{5,4},{6,7},{7,6},{8,9},{9,8},{10,11... | collective-permute-start | bytes 442376 | tf_op jit(solution)/shard_map/ppermute | solution.py:350
  70.0 7.5 %collective-permute-start.17 = (f32[768,384]{1,0:T(8,128)S(1)}, f32[768,384]{1,0:T(8,128)S(1)}, u32[]{:S(2)}, u32[]{:S(2)}) collective-permute-start(f32[768,384]{1,0:T(8,128)S(1)} %give_kernel.3.refs_0_), channel_id=1, source_target_pairs={{0,4},{4,0},{8,12},{12,8},{16,20},{20,16},{24,28},{28,24},{1,5},{5... | collective-permute-start | bytes 3538952 | tf_op jit(solution)/shard_map/ppermute | solution.py:337
  70.1 15.0 %collective-permute-start.19 = (f32[256,384]{1,0:T(8,128)S(1)}, f32[256,384]{1,0:T(8,128)S(1)}, u32[]{:S(2)}, u32[]{:S(2)}) collective-permute-start(f32[256,384]{1,0:T(8,128)S(1)} %get-tuple-element.33.refs_0_.refs_2_), channel_id=1, source_target_pairs={{0,8},{4,12},{24,16},{28,20},{1,9},{5,13},{25,17},{29,21},{2,10},{... | collective-permute-start | bytes 1179656 | tf_op jit(solution)/shard_map/ppermute | solution.py:341
  74.5 14.0 %collective-permute-start.20 = (f32[256,384]{1,0:T(8,128)S(1)}, f32[256,384]{1,0:T(8,128)S(1)}, u32[]{:S(2)}, u32[]{:S(2)}) collective-permute-start(f32[256,384]{1,0:T(8,128)S(1)} %add_kernel.21.refs_0_.refs_2_), channel_id=1, source_target_pairs={{8,16},{12,20},{16,8},{20,12},{9,17},{13,21},{17,9},{21,13},{10,18... | collective-permute-start | bytes 1179656 | tf_op jit(solution)/shard_map/ppermute | solution.py:341
  75.2 14.9 %collective-permute-start.21 = (f32[256,384]{1,0:T(8,128)S(1)}, f32[256,384]{1,0:T(8,128)S(1)}, u32[]{:S(2)}, u32[]{:S(2)}) collective-permute-start(f32[256,384]{1,0:T(8,128)S(1)} %add_kernel.23.refs_0_.refs_2_), channel_id=1, source_target_pairs={{8,16},{12,20},{16,8},{20,12},{9,17},{13,21},{17,9},{21,13},{10,18... | collective-permute-start | bytes 1179656 | tf_op jit(solution)/shard_map/ppermute | solution.py:341
  77.3 7.3 %collective-permute-start.18 = (f32[48,384]{1,0:T(8,128)S(1)}, f32[48,384]{1,0:T(8,128)S(1)}, u32[]{:S(2)}, u32[]{:S(2)}) collective-permute-start(f32[48,384]{1,0:T(8,128)S(1)} %get-tuple-element.42.refs_0_), channel_id=1, source_target_pairs={{0,4},{4,0},{8,12},{12,8},{16,20},{20,16},{24,28},{28,24},{1,5},{5... | collective-permute-start | bytes 221192 | tf_op jit(solution)/shard_map/ppermute | solution.py:337
  79.0 36.3 %collective-permute-start.25 = (f32[256,384]{1,0:T(8,128)S(1)}, f32[256,384]{1,0:T(8,128)S(1)}, u32[]{:S(2)}, u32[]{:S(2)}) collective-permute-start(f32[256,384]{1,0:T(8,128)S(1)} %get-tuple-element.45.refs_2_), channel_id=1, source_target_pairs={{0,8},{4,12},{24,16},{28,20},{1,9},{5,13},{25,17},{29,21},{2,10},{... | collective-permute-start | bytes 1179656 | tf_op jit(solution)/shard_map/ppermute | solution.py:341
  85.7 31.4 %collective-permute-start.26 = (f32[256,384]{1,0:T(8,128)S(1)}, f32[256,384]{1,0:T(8,128)S(1)}, u32[]{:S(2)}, u32[]{:S(2)}) collective-permute-start(f32[256,384]{1,0:T(8,128)S(1)} %add_kernel.26.refs_0_.refs_2_), channel_id=1, source_target_pairs={{8,16},{12,20},{16,8},{20,12},{9,17},{13,21},{17,9},{21,13},{10,18... | collective-permute-start | bytes 1179656 | tf_op jit(solution)/shard_map/ppermute | solution.py:341
  86.4 10.8 %collective-permute-start.22 = (f32[48,384]{1,0:T(8,128)S(1)}, f32[48,384]{1,0:T(8,128)S(1)}, u32[]{:S(2)}, u32[]{:S(2)}) collective-permute-start(f32[48,384]{1,0:T(8,128)S(1)} %add_kernel.25.refs_0_.refs_2_), channel_id=1, source_target_pairs={{0,8},{4,12},{8,16},{12,20},{16,24},{20,28},{24,0},{28,4},{1,9},{5... | collective-permute-start | bytes 221192 | tf_op jit(solution)/shard_map/ppermute | solution.py:341
  88.6 20.2 %collective-permute-start.23 = (f32[48,384]{1,0:T(8,128)S(1)}, f32[48,384]{1,0:T(8,128)S(1)}, u32[]{:S(2)}, u32[]{:S(2)}) collective-permute-start(f32[48,384]{1,0:T(8,128)S(1)} %add_kernel.25.refs_0_.refs_2_), channel_id=1, source_target_pairs={{0,16},{4,20},{8,24},{12,28},{16,0},{20,4},{24,8},{28,12},{1,17},{... | collective-permute-start | bytes 221192 | tf_op jit(solution)/shard_map/ppermute | solution.py:341
  90.1 18.6 %collective-permute-start.24 = (f32[48,384]{1,0:T(8,128)S(1)}, f32[48,384]{1,0:T(8,128)S(1)}, u32[]{:S(2)}, u32[]{:S(2)}) collective-permute-start(f32[48,384]{1,0:T(8,128)S(1)} %add_kernel.25.refs_0_.refs_2_), channel_id=1, source_target_pairs={{0,24},{4,28},{8,0},{12,4},{16,8},{20,12},{24,16},{28,20},{1,25},{... | collective-permute-start | bytes 221192 | tf_op jit(solution)/shard_map/ppermute | solution.py:341
  109.3 13.1 %collective-permute-start.27 = (f32[48,384]{1,0:T(8,128)S(1)}, f32[48,384]{1,0:T(8,128)S(1)}, u32[]{:S(2)}, u32[]{:S(2)}) collective-permute-start(f32[48,384]{1,0:T(8,128)S(1)} %total_kernel.1.refs_0_.refs_2_), channel_id=1, source_target_pairs={{0,4},{4,0},{8,12},{12,8},{16,20},{20,16},{24,28},{28,24},{1,5},{5... | collective-permute-start | bytes 221192 | tf_op jit(solution)/shard_map/ppermute | solution.py:337
  109.4 14.9 %collective-permute-start.28 = (f32[256,384]{1,0:T(8,128)S(1)}, f32[256,384]{1,0:T(8,128)S(1)}, u32[]{:S(2)}, u32[]{:S(2)}) collective-permute-start(f32[256,384]{1,0:T(8,128)S(1)} %add_kernel.27.refs_0_.refs_2_), channel_id=1, source_target_pairs={{8,0},{12,4},{16,24},{20,28},{9,1},{13,5},{17,25},{21,29},{10,2},{... | collective-permute-start | bytes 1179656 | tf_op jit(solution)/shard_map/ppermute | solution.py:341
  110.7 14.2 %collective-permute-start.29 = (f32[256,384]{1,0:T(8,128)S(1)}, f32[256,384]{1,0:T(8,128)S(1)}, u32[]{:S(2)}, u32[]{:S(2)}) collective-permute-start(f32[256,384]{1,0:T(8,128)S(1)} %get-tuple-element.46.refs_2_), channel_id=1, source_target_pairs={{0,8},{4,12},{24,16},{28,20},{1,9},{5,13},{25,17},{29,21},{2,10},{... | collective-permute-start | bytes 1179656 | tf_op jit(solution)/shard_map/ppermute | solution.py:341
  115.3 16.3 %collective-permute-start.30 = (f32[256,384]{1,0:T(8,128)S(1)}, f32[256,384]{1,0:T(8,128)S(1)}, u32[]{:S(2)}, u32[]{:S(2)}) collective-permute-start(f32[256,384]{1,0:T(8,128)S(1)} %add_kernel.28.refs_0_.refs_2_), channel_id=1, source_target_pairs={{8,0},{12,4},{16,24},{20,28},{9,1},{13,5},{17,25},{21,29},{10,2},{... | collective-permute-start | bytes 1179656 | tf_op jit(solution)/shard_map/ppermute | solution.py:341
  117.2 15.2 %collective-permute-start.31 = (f32[256,384]{1,0:T(8,128)S(1)}, f32[256,384]{1,0:T(8,128)S(1)}, u32[]{:S(2)}, u32[]{:S(2)}) collective-permute-start(f32[256,384]{1,0:T(8,128)S(1)} %get-tuple-element.43.refs_0_.refs_2_), channel_id=1, source_target_pairs={{0,8},{4,12},{24,16},{28,20},{1,9},{5,13},{25,17},{29,21},{2,10},{... | collective-permute-start | bytes 1179656 | tf_op jit(solution)/shard_map/ppermute | solution.py:341
  122.4 17.2 %collective-permute-start.32 = (f32[256,384]{1,0:T(8,128)S(1)}, f32[256,384]{1,0:T(8,128)S(1)}, u32[]{:S(2)}, u32[]{:S(2)}) collective-permute-start(f32[256,384]{1,0:T(8,128)S(1)} %add_kernel.30.refs_0_.refs_2_), channel_id=1, source_target_pairs={{8,0},{12,4},{16,24},{20,28},{9,1},{13,5},{17,25},{21,29},{10,2},{... | collective-permute-start | bytes 1179656 | tf_op jit(solution)/shard_map/ppermute | solution.py:341
  142.8 1.8 collective-permute-start.33
  142.9 2.9 %collective-permute-start.35 = (f32[256,384]{1,0:T(8,128)S(1)}, f32[256,384]{1,0:T(8,128)S(1)}, u32[]{:S(2)}, u32[]{:S(2)}) collective-permute-start(f32[256,384]{1,0:T(8,128)S(1)} %pick_kernel.7.refs_0_.refs_3_.refs_5_), channel_id=1, source_target_pairs={{0,4},{4,0},{8,12},{12,8},{16,20},{20,16},{24,28},{28,24},{1,5},{5... | collective-permute-start | bytes 1179656 | tf_op jit(solution)/shard_map/ppermute | solution.py:337
  143.4 3.1 %collective-permute-start.34 = (f32[256,384]{1,0:T(8,128)S(1)}, f32[256,384]{1,0:T(8,128)S(1)}, u32[]{:S(2)}, u32[]{:S(2)}) collective-permute-start(f32[256,384]{1,0:T(8,128)S(1)} %pick_kernel.6.refs_0_.refs_2_.refs_4_), channel_id=1, source_target_pairs={{0,4},{4,0},{8,12},{12,8},{16,20},{20,16},{24,28},{28,24},{1,5},{5... | collective-permute-start | bytes 1179656 | tf_op jit(solution)/shard_map/ppermute | solution.py:337
  143.5 3.7 %collective-permute-start.36 = (f32[256,384]{1,0:T(8,128)S(1)}, f32[256,384]{1,0:T(8,128)S(1)}, u32[]{:S(2)}, u32[]{:S(2)}) collective-permute-start(f32[256,384]{1,0:T(8,128)S(1)} %pick_kernel.8.refs_0_.refs_4_.refs_6_), channel_id=1, source_target_pairs={{0,4},{4,0},{8,12},{12,8},{16,20},{20,16},{24,28},{28,24},{1,5},{5... | collective-permute-start | bytes 1179656 | tf_op jit(solution)/shard_map/ppermute | solution.py:337
  143.9 6.6 %collective-permute-start.37 = (f32[256,384]{1,0:T(8,128)S(1)}, f32[256,384]{1,0:T(8,128)S(1)}, u32[]{:S(2)}, u32[]{:S(2)}) collective-permute-start(f32[256,384]{1,0:T(8,128)S(1)} %add_kernel.29.refs_0_.refs_2_), channel_id=1, source_target_pairs={{8,16},{12,20},{16,8},{20,12},{9,17},{13,21},{17,9},{21,13},{10,18... | collective-permute-start | bytes 1179656 | tf_op jit(solution)/shard_map/ppermute | solution.py:341
  145.2 9.9 %collective-permute-start.38 = (f32[192,384]{1,0:T(8,128)S(1)}, f32[192,384]{1,0:T(8,128)S(1)}, u32[]{:S(2)}, u32[]{:S(2)}) collective-permute-start(f32[192,384]{1,0:T(8,128)S(1)} %add_kernel.33.refs_0_.refs_2_), channel_id=1, source_target_pairs={{0,1},{1,0},{2,3},{3,2},{4,5},{5,4},{6,7},{7,6},{8,9},{9,8},{10,11... | collective-permute-start | bytes 884744 | tf_op jit(solution)/shard_map/ppermute | solution.py:350
  145.8 13.3 %collective-permute-start.41 = (f32[256,384]{1,0:T(8,128)S(1)}, f32[256,384]{1,0:T(8,128)S(1)}, u32[]{:S(2)}, u32[]{:S(2)}) collective-permute-start(f32[256,384]{1,0:T(8,128)S(1)} %add_kernel.31.refs_0_.refs_2_), channel_id=1, source_target_pairs={{8,16},{12,20},{16,8},{20,12},{9,17},{13,21},{17,9},{21,13},{10,18... | collective-permute-start | bytes 1179656 | tf_op jit(solution)/shard_map/ppermute | solution.py:341
  146.5 21.9 %collective-permute-start.45 = (f32[256,384]{1,0:T(8,128)S(1)}, f32[256,384]{1,0:T(8,128)S(1)}, u32[]{:S(2)}, u32[]{:S(2)}) collective-permute-start(f32[256,384]{1,0:T(8,128)S(1)} %add_kernel.32.refs_0_.refs_2_), channel_id=1, source_target_pairs={{8,16},{12,20},{16,8},{20,12},{9,17},{13,21},{17,9},{21,13},{10,18... | collective-permute-start | bytes 1179656 | tf_op jit(solution)/shard_map/ppermute | solution.py:341
  149.0 8.5 %collective-permute-start.39 = (f32[96,384]{1,0:T(8,128)S(1)}, f32[96,384]{1,0:T(8,128)S(1)}, u32[]{:S(2)}, u32[]{:S(2)}) collective-permute-start(f32[96,384]{1,0:T(8,128)S(1)} %get-tuple-element.50.refs_2_), channel_id=1, source_target_pairs={{0,1},{1,0},{2,3},{3,2},{4,5},{5,4},{6,7},{7,6},{8,9},{9,8},{10,11... | collective-permute-start | bytes 442376 | tf_op jit(solution)/shard_map/ppermute | solution.py:350
  150.5 6.9 %collective-permute-start.40 = (f32[96,384]{1,0:T(8,128)S(1)}, f32[96,384]{1,0:T(8,128)S(1)}, u32[]{:S(2)}, u32[]{:S(2)}) collective-permute-start(f32[96,384]{1,0:T(8,128)S(1)} %get-tuple-element.49.refs_0_.refs_4_), channel_id=1, source_target_pairs={{0,2},{1,3},{2,0},{3,1},{4,6},{5,7},{6,4},{7,5},{8,10},{9,11},{10,... | collective-permute-start | bytes 442376 | tf_op jit(solution)/shard_map/ppermute | solution.py:350
  155.7 8.9 %collective-permute-start.42 = (f32[192,384]{1,0:T(8,128)S(1)}, f32[192,384]{1,0:T(8,128)S(1)}, u32[]{:S(2)}, u32[]{:S(2)}) collective-permute-start(f32[192,384]{1,0:T(8,128)S(1)} %add_kernel.35.refs_0_.refs_2_), channel_id=1, source_target_pairs={{0,2},{1,3},{2,0},{3,1},{4,6},{5,7},{6,4},{7,5},{8,10},{9,11},{10,... | collective-permute-start | bytes 884744 | tf_op jit(solution)/shard_map/ppermute | solution.py:350
  158.0 8.5 %collective-permute-start.43 = (f32[96,384]{1,0:T(8,128)S(1)}, f32[96,384]{1,0:T(8,128)S(1)}, u32[]{:S(2)}, u32[]{:S(2)}) collective-permute-start(f32[96,384]{1,0:T(8,128)S(1)} %get-tuple-element.52.refs_2_), channel_id=1, source_target_pairs={{0,2},{1,3},{2,0},{3,1},{4,6},{5,7},{6,4},{7,5},{8,10},{9,11},{10,... | collective-permute-start | bytes 442376 | tf_op jit(solution)/shard_map/ppermute | solution.py:350
  158.6 9.2 %collective-permute-start.44 = (f32[96,384]{1,0:T(8,128)S(1)}, f32[96,384]{1,0:T(8,128)S(1)}, u32[]{:S(2)}, u32[]{:S(2)}) collective-permute-start(f32[96,384]{1,0:T(8,128)S(1)} %get-tuple-element.51.refs_0_.refs_4_), channel_id=1, source_target_pairs={{0,1},{1,0},{2,3},{3,2},{4,5},{5,4},{6,7},{7,6},{8,9},{9,8},{10,11... | collective-permute-start | bytes 442376 | tf_op jit(solution)/shard_map/ppermute | solution.py:350
  159.2 11.9 %collective-permute-start.46 = (f32[96,384]{1,0:T(8,128)S(1)}, f32[96,384]{1,0:T(8,128)S(1)}, u32[]{:S(2)}, u32[]{:S(2)}) collective-permute-start(f32[96,384]{1,0:T(8,128)S(1)} %order_kernel.1.refs_0_.refs_2_), channel_id=1, source_target_pairs={{0,1},{1,0},{2,3},{3,2},{4,5},{5,4},{6,7},{7,6},{8,9},{9,8},{10,11... | collective-permute-start | bytes 442376 | tf_op jit(solution)/shard_map/ppermute | solution.py:350
  164.6 34.4 %collective-permute-start.50 = (f32[256,384]{1,0:T(8,128)S(1)}, f32[256,384]{1,0:T(8,128)S(1)}, u32[]{:S(2)}, u32[]{:S(2)}) collective-permute-start(f32[256,384]{1,0:T(8,128)S(1)} %add_kernel.34.refs_0_.refs_2_), channel_id=1, source_target_pairs={{8,0},{12,4},{16,24},{20,28},{9,1},{13,5},{17,25},{21,29},{10,2},{... | collective-permute-start | bytes 1179656 | tf_op jit(solution)/shard_map/ppermute | solution.py:341
  166.5 33.2 %collective-permute-start.51 = (f32[256,384]{1,0:T(8,128)S(1)}, f32[256,384]{1,0:T(8,128)S(1)}, u32[]{:S(2)}, u32[]{:S(2)}) collective-permute-start(f32[256,384]{1,0:T(8,128)S(1)} %add_kernel.37.refs_0_.refs_2_), channel_id=1, source_target_pairs={{8,0},{12,4},{16,24},{20,28},{9,1},{13,5},{17,25},{21,29},{10,2},{... | collective-permute-start | bytes 1179656 | tf_op jit(solution)/shard_map/ppermute | solution.py:341
  169.0 31.9 %collective-permute-start.52 = (f32[256,384]{1,0:T(8,128)S(1)}, f32[256,384]{1,0:T(8,128)S(1)}, u32[]{:S(2)}, u32[]{:S(2)}) collective-permute-start(f32[256,384]{1,0:T(8,128)S(1)} %add_kernel.40.refs_0_.refs_2_), channel_id=1, source_target_pairs={{8,0},{12,4},{16,24},{20,28},{9,1},{13,5},{17,25},{21,29},{10,2},{... | collective-permute-start | bytes 1179656 | tf_op jit(solution)/shard_map/ppermute | solution.py:341
  170.5 6.8 %collective-permute-start.47 = (f32[96,384]{1,0:T(8,128)S(1)}, f32[96,384]{1,0:T(8,128)S(1)}, u32[]{:S(2)}, u32[]{:S(2)}) collective-permute-start(f32[96,384]{1,0:T(8,128)S(1)} %order_kernel.1.refs_0_.refs_2_), channel_id=1, source_target_pairs={{0,2},{1,3},{2,0},{3,1},{4,6},{5,7},{6,4},{7,5},{8,10},{9,11},{10,... | collective-permute-start | bytes 442376 | tf_op jit(solution)/shard_map/ppermute | solution.py:350
  171.1 12.3 %collective-permute-start.49 = (f32[192,384]{1,0:T(8,128)S(1)}, f32[192,384]{1,0:T(8,128)S(1)}, u32[]{:S(2)}, u32[]{:S(2)}) collective-permute-start(f32[192,384]{1,0:T(8,128)S(1)} %add_kernel.38.refs_0_.refs_6_), channel_id=1, source_target_pairs={{0,4},{4,0},{8,12},{12,8},{16,20},{20,16},{24,28},{28,24},{1,5},{5... | collective-permute-start | bytes 884744 | tf_op jit(solution)/shard_map/ppermute | solution.py:337
  177.3 6.0 %collective-permute-start.48 = (f32[96,384]{1,0:T(8,128)S(1)}, f32[96,384]{1,0:T(8,128)S(1)}, u32[]{:S(2)}, u32[]{:S(2)}) collective-permute-start(f32[96,384]{1,0:T(8,128)S(1)} %order_kernel.1.refs_0_.refs_2_), channel_id=1, source_target_pairs={{0,3},{1,2},{2,1},{3,0},{4,7},{5,6},{6,5},{7,4},{8,11},{9,10},{10,... | collective-permute-start | bytes 442376 | tf_op jit(solution)/shard_map/ppermute | solution.py:350
  199.7 4.7 %collective-permute-start.53 = (f32[256,384]{1,0:T(8,128)S(1)}, f32[256,384]{1,0:T(8,128)S(1)}, u32[]{:S(2)}, u32[]{:S(2)}) collective-permute-start(f32[256,384]{1,0:T(8,128)S(1)} %pick_kernel.9.refs_0_.refs_2_), channel_id=1, source_target_pairs={{0,4},{4,0},{8,12},{12,8},{16,20},{20,16},{24,28},{28,24},{1,5},{5... | collective-permute-start | bytes 1179656 | tf_op jit(solution)/shard_map/ppermute | solution.py:337
  200.4 4.0 %collective-permute-start.54 = (f32[256,384]{1,0:T(8,128)S(1)}, f32[256,384]{1,0:T(8,128)S(1)}, u32[]{:S(2)}, u32[]{:S(2)}) collective-permute-start(f32[256,384]{1,0:T(8,128)S(1)} %pick_kernel.10.refs_0_.refs_3_), channel_id=1, source_target_pairs={{0,4},{4,0},{8,12},{12,8},{16,20},{20,16},{24,28},{28,24},{1,5},{5... | collective-permute-start | bytes 1179656 | tf_op jit(solution)/shard_map/ppermute | solution.py:337
  201.5 2.8 %collective-permute-start.55 = (f32[256,384]{1,0:T(8,128)S(1)}, f32[256,384]{1,0:T(8,128)S(1)}, u32[]{:S(2)}, u32[]{:S(2)}) collective-permute-start(f32[256,384]{1,0:T(8,128)S(1)} %pick_kernel.11.refs_0_.refs_4_), channel_id=1, source_target_pairs={{0,4},{4,0},{8,12},{12,8},{16,20},{20,16},{24,28},{28,24},{1,5},{5... | collective-permute-start | bytes 1179656 | tf_op jit(solution)/shard_map/ppermute | solution.py:337
  203.9 4.8 %collective-permute-start.56 = (f32[1,384]{1,0:T(1,128)S(1)}, f32[1,384]{1,0:T(1,128)S(1)}, u32[]{:S(2)}, u32[]{:S(2)}) collective-permute-start(f32[1,384]{1,0:T(1,128)S(1)} %get-tuple-element.56.refs_0_.refs_2_), channel_id=1, source_target_pairs={{0,4},{4,0},{8,12},{12,8},{16,20},{20,16},{24,28},{28,24},{1,5},{5... | collective-permute-start | bytes 4616 | tf_op jit(solution)/shard_map/ppermute | solution.py:337
  209.2 22.0 %collective-permute-start.60 = (f32[1,384]{1,0:T(1,128)S(1)}, f32[1,384]{1,0:T(1,128)S(1)}, u32[]{:S(2)}, u32[]{:S(2)}) collective-permute-start(f32[1,384]{1,0:T(1,128)S(1)} %add_kernel.41.refs_0_), channel_id=1, source_target_pairs={{0,8},{4,12},{8,16},{12,20},{16,24},{20,28},{24,0},{28,4},{1,9},{5... | collective-permute-start | bytes 4616 | tf_op jit(solution)/shard_map/ppermute | solution.py:341
  212.7 20.2 %collective-permute-start.61 = (f32[1,384]{1,0:T(1,128)S(1)}, f32[1,384]{1,0:T(1,128)}, u32[]{:S(2)}, u32[]{:S(2)}) collective-permute-start(f32[1,384]{1,0:T(1,128)S(1)} %add_kernel.41.refs_0_), channel_id=1, source_target_pairs={{0,16},{4,20},{8,24},{12,28},{16,0},{20,4},{24,8},{28,12},{1,17},{... | collective-permute-start | bytes 4616 | tf_op jit(solution)/shard_map/ppermute | solution.py:341
  213.6 19.3 %collective-permute-start.62 = (f32[1,384]{1,0:T(1,128)S(1)}, f32[1,384]{1,0:T(1,128)}, u32[]{:S(2)}, u32[]{:S(2)}) collective-permute-start(f32[1,384]{1,0:T(1,128)S(1)} %add_kernel.41.refs_0_), channel_id=1, source_target_pairs={{0,24},{4,28},{8,0},{12,4},{16,8},{20,12},{24,16},{28,20},{1,25},{... | collective-permute-start | bytes 4616 | tf_op jit(solution)/shard_map/ppermute | solution.py:341
  216.4 18.7 %collective-permute-start.57 = (f32[1,384]{1,0:T(1,128)S(1)}, f32[1,384]{1,0:T(1,128)S(1)}, u32[]{:S(2)}, u32[]{:S(2)}) collective-permute-start(f32[1,384]{1,0:T(1,128)S(1)} %get-tuple-element.58.refs_0_), channel_id=1, source_target_pairs={{0,1},{1,0},{2,3},{3,2},{4,5},{5,4},{6,7},{7,6},{8,9},{9,8},{10,11... | collective-permute-start | bytes 4616 | tf_op jit(solution)/shard_map/ppermute | solution.py:350
  217.0 18.2 %collective-permute-start.58 = (f32[1,384]{1,0:T(1,128)S(1)}, f32[1,384]{1,0:T(1,128)S(1)}, u32[]{:S(2)}, u32[]{:S(2)}) collective-permute-start(f32[1,384]{1,0:T(1,128)S(1)} %get-tuple-element.58.refs_0_), channel_id=1, source_target_pairs={{0,2},{1,3},{2,0},{3,1},{4,6},{5,7},{6,4},{7,5},{8,10},{9,11},{10,... | collective-permute-start | bytes 4616 | tf_op jit(solution)/shard_map/ppermute | solution.py:350
  231.2 4.5 %collective-permute-start.59 = (f32[1,384]{1,0:T(1,128)S(1)}, f32[1,384]{1,0:T(1,128)S(1)}, u32[]{:S(2)}, u32[]{:S(2)}) collective-permute-start(f32[1,384]{1,0:T(1,128)S(1)} %get-tuple-element.58.refs_0_), channel_id=1, source_target_pairs={{0,3},{1,2},{2,1},{3,0},{4,7},{5,6},{6,5},{7,4},{8,11},{9,10},{10,... | collective-permute-start | bytes 4616 | tf_op jit(solution)/shard_map/ppermute | solution.py:350
  (26 other events, 81.0 us)

commit v2 on v1

--- a/solution.py
+++ b/solution.py
@@ -43,8 +43,9 @@
         self.place = jnp.stack((lax.axis_index("col"), z, core)).astype(jnp.int32)
         self.last = ()
 
-    def __call__(self, kernel, outs, *args, scratch=()):
-        last = len(self.last)
+    def __call__(self, kernel, outs, *args, scratch=(), wait=()):
+        waits = self.last + tuple(wait)
+        last = len(waits)
         whole = pl.BlockSpec(memory_space=pltpu.VMEM)
 
         def body(*refs):
@@ -58,10 +59,10 @@
             + [whole] * len(args),
             out_specs=[whole] * len(outs),
             scratch_shapes=[pltpu.VMEM(shape, jnp.float32) for shape in scratch],
-            compiler_params=pltpu.CompilerParams(vmem_limit_bytes=24 * 2**20),
+            compiler_params=pltpu.CompilerParams(vmem_limit_bytes=16 * 2**20),
             cost_estimate=free,
             name=getattr(kernel, "func", kernel).__name__,
-        )(*self.last, self.place, *args)
+        )(*waits, self.place, *args)
         self.last = (results[-1],)
         return results
 
@@ -164,15 +165,17 @@
                 outs[m][at(i), at(j)] = inverse[i, j] if j <= i else jnp.zeros((tile, tile), jnp.float32)
 
 
-def inverse_kernel(place, *refs):
-    *stripes, mine, other, out_one, out_two, gram_one, gram_two = refs
-    col, core = place[0], place[2]
+def gather_kernel(place, *refs):
+    *stripes, out = refs
     rows = stripes[0].shape[0]
     for bits, stripe in enumerate(stripes):
-        gram_one[pl.ds(pl.multiple_of((col ^ bits) * rows, 8), rows), :] = stripe[...]
+        out[pl.ds(pl.multiple_of((place[0] ^ bits) * rows, 8), rows), :] = stripe[...]
+
+
+def inverse_kernel(place, gram_one, mine, other, out_one, out_two, gram_two):
     half = mine.shape[0]
-    gram_two[pl.ds(pl.multiple_of(core * half, 8), half), :] = mine[...]
-    gram_two[pl.ds(pl.multiple_of((1 - core) * half, 8), half), :] = other[...]
+    gram_two[pl.ds(pl.multiple_of(place[2] * half, 8), half), :] = mine[...]
+    gram_two[pl.ds(pl.multiple_of((1 - place[2]) * half, 8), half), :] = other[...]
     inverse_blocks((gram_one, gram_two), (out_one, out_two))
 
 
@@ -225,25 +228,15 @@
     out[...] = jnp.concatenate((jnp.where(first, a, b), jnp.where(first, b, a)), axis=0)
 
 
-def stack_kernel(place, own, *refs):
-    *moved, out = refs
-    count = len(moved) // 2
-    up, down = moved[:count], moved[count:]
-    rows = own.shape[0]
-    out[:rows, :] = own[...]
-    for s in range(1, count + 1):
-        out[s * rows : (s + 1) * rows, :] = up[count - s][...] + down[s - 1][...]
-
-
-def first_panel(line, place, moment, gradient, mine, other, low, high):
+def first_panel(line, place, moment, gradient, *refs):
+    mine, other, (low, high) = refs[:line], refs[line : 2 * line], refs[2 * line :]
     width = moment.shape[1] // line
-    rows = width // 2
     first = place[2] == 0
     total = None
     for s in range(line):
         at = many(lax.rem(place[1] + s, line) * width, width)
         buffer = moment[:, at] + gradient[:, at].astype(jnp.float32)
-        a, b = mine[s * rows : (s + 1) * rows, :], other[s * rows : (s + 1) * rows, :]
+        a, b = mine[s][...], other[s][...]
         factor = jnp.concatenate((jnp.where(first, a, b), jnp.where(first, b, a)), axis=0)
         term = product_split(buffer, factor, 1, 0)
         total = term if total is None else total + term
@@ -352,12 +345,17 @@
 
 def gather_line(flow, x):
     line = line_size()
-    up, down = [x], [x]
+    up, down, mine, other = [x], [x], {0: x}, {0: swap_core(x)}
     for s in range(1, line):
         up.append(move_line(up[-1], [(z, z + 1) for z in range(s - 1, line - 1)]))
         down.append(move_line(down[-1], [(z, z - 1) for z in range(1, line - s + 1)]))
-    mine = flow(stack_kernel, [(line * x.shape[0], x.shape[1])], *up, *down[1:])[0]
-    return mine, swap_core(mine)
+        yield up[-1], down[-1]
+        ready = [k for k in range(1, line) if max(k, line - k) == s]
+        if ready:
+            pairs = [y for k in ready for y in (up[line - k], down[k])]
+            for k, y in zip(ready, flow(add_kernel, [x.shape] * len(ready), *pairs)):
+                mine[k], other[k] = y, swap_core(y)
+    return [mine[k] for k in range(line)] + [other[k] for k in range(line)]
 
 
 def sum_line(flow, x):
@@ -418,7 +416,9 @@
     moved = swap_core(part)
     yield
     stripe = flow(order_kernel, [(2 * shape[0], size)], part, moved)[0]
-    return [stripe] + [swap_col(stripe, bits) for bits in range(1, cols)]
+    moved = [swap_col(stripe, bits) for bits in range(1, cols)]
+    yield
+    return flow(gather_kernel, [(size, size)], stripe, *moved)[0]
 
 
 def gram_halves(flow, parts):
@@ -435,14 +435,19 @@
     return [part, swap_core(part)]
 
 
-def sum_squares(flow, right, left):
-    moved = [swap_col(right, b) for b in range(1, lax.axis_size("col"))]
+def sum_left(flow, left):
     came = swap_core(left)
     yield
     left = flow(add_kernel, [left.shape], left, came)[0]
     turned = [turn_line(left, s) for s in range(1, line_size())]
     yield
-    return functools.reduce(jnp.add, moved, right), functools.reduce(jnp.add, turned, left)
+    return flow(total_kernel, [left.shape], left, *turned)[0]
+
+
+def sum_right(flow, right):
+    moved = [swap_col(right, b) for b in range(1, lax.axis_size("col"))]
+    yield
+    return flow(total_kernel, [right.shape], right, *moved)[0]
 
 
 def shards(moment_one, gradient_one, factor_one, moment_two, gradient_two, factor_two):
@@ -461,39 +466,44 @@
     block = (local_rows, rank)
     square = (rank, rank)
 
-    def transposed(buffer, *parts):
-        came = swap_core(flow(give_kernel, [half], *buffer, *parts)[0])
+    def transposed(buffer, *parts, wait=()):
+        came = swap_core(flow(give_kernel, [half], *buffer, *parts, wait=wait)[0])
         yield
         kernel = functools.partial(keep_kernel, len(parts))
         values = flow(kernel, [chunk] * chunks, *buffer, came, *parts)
         return [Task(sum_line(flow, value)).step() for value in values]
 
-    panel_two = Task(transposed(two, gather_col(factor_two))).step().finish()
-
-    factor = gather_line(flow, factor_one)
+    gather = gather_line(flow, factor_one)
+    came = next(gather)
+    factor = Task(gather).step()
+    panel_two = Task(transposed(two, gather_col(factor_two), wait=came)).step()
+    panel_two = panel_two.finish()
+    factor.step()
+    panel_two[0].step()
+    factor = factor.finish()
+
     panel_one = flow(functools.partial(first_panel, line), low_high, *one, *factor)
     panel_one = Task(sum_col(flow, *panel_one)).step()
+    panel_two[1].step()
+    panel_one.step()
+    panel_two[2].step()
     panel_two[0].step()
-    panel_one.step()
+    panel_one = panel_one.finish()
+
+    gram_one = Task(gram_stripes(flow, *panel_one)).step()
+    right = Task(transposed(one, *panel_one)).step()
+    gram_one.step()
+    right = right.finish()
     panel_two[1].step()
-    panel_one = panel_one.finish()
-
-    right = Task(transposed(one, *panel_one)).step()
-    gram_one = Task(gram_stripes(flow, *panel_one)).step()
-    right = right.finish()
+    panel_two[0].finish()
     gram_one.step()
     panel_two[2].step()
-    panel_two[0].step()
-    panel_two[1].step()
     gram_one.step()
     right[0].step()
-    panel_two[2].step()
+    panel_two[1].finish()
     gram_one = gram_one.finish()
-    panel_two[0].finish()
+    panel_two[2].finish()
     right[1].step()
-    panel_two[1].finish()
-    right[2].step()
-    panel_two[2].finish()
 
     panel_two = [part for task in panel_two for part in task.result]
     panel_two = panel_two[::2] + panel_two[1::2]
@@ -501,6 +511,7 @@
     left = flow(functools.partial(second_product, chunks), low_high, *two, *panel_two)
     left = Task(sum_col(flow, *left)).step()
     right[0].step()
+    right[2].step()
     gram_two.step()
     left.step()
     right[1].step()
@@ -508,20 +519,23 @@
     left = left.finish()
     right[2].step()
 
-    inverse_one, inverse_two = flow(
-        inverse_kernel, [square, square], *gram_one, *gram_two, scratch=[square, square]
-    )
-    right = [part for task in right for part in task.finish()]
+    inverse_one, inverse_two = flow(inverse_kernel, [square, square], gram_one, *gram_two, scratch=[square])
+
+    for task in right:
+        task.finish()
+    left_sum, weight_two, squares_left = flow(left_kernel, [block, block, (1, rank)], *left, inverse_two)
+    squares_left = Task(sum_left(flow, squares_left)).step()
+    right = [part for task in right for part in task.result]
     right = right[::2] + right[1::2]
-
-    left_sum, weight_two, squares_left = flow(left_kernel, [block, block, (1, rank)], *left, inverse_two)
     kernel = functools.partial(right_kernel, chunks)
     right_sum, squares_right = flow(kernel, [(local_cols, rank), (1, rank)], *right, inverse_one)
-    squares = Task(sum_squares(flow, squares_right, squares_left)).step(2)
+    squares_right = Task(sum_right(flow, squares_right)).step()
+    squares_left.step()
     kernel = functools.partial(carry_two_kernel, chunks)
     carried_two = flow(kernel, [moment_two.shape], *two, *panel_two, weight_two)[0]
+    squares_right = squares_right.finish()
     carried_one = flow(carry_one_kernel, [moment_one.shape], *one, *panel_one, inverse_one, right_sum)[0]
-    squares_right, squares_left = squares.finish()
+    squares_left = squares_left.finish()
 
     right_rows = local_cols // (2 * line)
     right_part = rows_at(right_sum, lax.axis_index("row") * right_rows, right_rows)

time: 237 us -> 216 us (0.911)
  waiting for transfers between devices: 87.2 us -> 45.8 us
  starting transfers between devices: 76.5 us -> 93.5 us
  Pallas kernels: 57.4 us -> 59.8 us
    ppermute x30, waiting for transfers between devices: 61.9 us -> 30.3 us  [move_line(): lax.ppermute(x, 'row', [(2 * a + k, 2 * b + k) for a, b in pairs for k in...]
    ppermute x19, waiting for transfers between devices: 25.3 us -> 10.9 us  [swap_col(): lax.ppermute(x, 'col', [(i, i ^ bits) for i in range(lax.axis_size('col'))])]
    ppermute x30, starting transfers between devices: 56.4 us -> 65.4 us  [move_line(): lax.ppermute(x, 'row', [(2 * a + k, 2 * b + k) for a, b in pairs for k in...]
    ppermute x19, starting transfers between devices: 17.3 us -> 23.8 us  [swap_col(): lax.ppermute(x, 'col', [(i, i ^ bits) for i in range(lax.axis_size('col'))])]
    ppermute x14 -> x17, waiting for transfers between devices: 0.07 us -> 4.62 us  [swap_core(): lax.ppermute(x, 'row', [(i, i ^ 1) for i in range(lax.axis_size('row'))])]
    pallas_call x43 -> x47, Pallas kernels: 57.4 us -> 59.8 us  [__call__(): pl.pallas_call(body, out_shape=[jax.ShapeDtypeStruct(shape, jnp.float32)...]
    unnamed x54 -> x56, local copies, waits for them, and re-layouts: 9.71 us -> 11 us
  transfers between devices with their start and end apart: 63 -> 66, of which waited for: 20 -> 20; matrix products, arithmetic and copies ran while one was open for 1% -> 0% of each run, Pallas kernels for 21% -> 24%
where the time goes in v2:
time: 216 us; the launch traced here: 215 us
  starting transfers between devices  93.5 us (43%)
  Pallas kernels  59.8 us (28%)
  waiting for transfers between devices  45.8 us (21%)
  local copies, waits for them, and re-layouts  12 us (6%)
  other arithmetic  2.39 us (1%)
    ppermute x30, starting transfers between devices, move_line(): lax.ppermute(x, 'row', [(2 * a + k, 2 * b + k) for a, b in pairs for k in...  65.4 us
    pallas_call x47, Pallas kernels, __call__(): pl.pallas_call(body, out_shape=[jax.ShapeDtypeStruct(shape, jnp.float32)...  59.8 us
    ppermute x30, waiting for transfers between devices, move_line(): lax.ppermute(x, 'row', [(2 * a + k, 2 * b + k) for a, b in pairs for k in...  30.3 us
    ppermute x19, starting transfers between devices, swap_col(): lax.ppermute(x, 'col', [(i, i ^ bits) for i in range(lax.axis_size('col'))])  23.8 us
    unnamed x56, local copies, waits for them, and re-layouts  11 us
    ppermute x19, waiting for transfers between devices, swap_col(): lax.ppermute(x, 'col', [(i, i ^ bits) for i in range(lax.axis_size('col'))])  10.9 us
    ppermute x17, waiting for transfers between devices, swap_core(): lax.ppermute(x, 'row', [(i, i ^ 1) for i in range(lax.axis_size('row'))])  4.62 us
  transfers between devices with their start and end apart: 66, of which 20 were waited for; matrix products, arithmetic and copies ran while one was open for 0% of the time, Pallas kernels for 24%

profile of v2, /device:TPU:0, one launch (start us, length us, event | category | flops | bytes accessed | tf_op | source)
XLA Modules:
  0.0 215.2 jit_solution(8012321286683312328)
XLA Ops:
  0.6 3.0 %collective-permute-start.2 = (f32[48,384]{1,0:T(8,128)}, f32[48,384]{1,0:T(8,128)S(1)}, u32[]{:S(2)}, u32[]{:S(2)}) collective-permute-start(f32[48,384]{1,0:T(8,128)} %param.11), channel_id=1, source_target_pairs={{0,1},{1,0},{2,3},{3,2},{4,5},{5,4},{6,7},{7,6},{8,9},{9,8},{10,11... | collective-permute-start | bytes 221192 | tf_op jit(solution)/shard_map/ppermute | solution.py:343
  3.6 1.5 collective-permute-start.3
  5.2 3.9 %collective-permute-start = (f32[192,384]{1,0:T(8,128)}, f32[192,384]{1,0:T(8,128)S(1)}, u32[]{:S(2)}, u32[]{:S(2)}) collective-permute-start(f32[192,384]{1,0:T(8,128)} %refs_4_.3), channel_id=1, source_target_pairs={{0,8},{4,12},{8,16},{12,20},{16,24},{20,28},{1,9},{5,13},{9,17},{1... | collective-permute-start | bytes 884744 | tf_op jit(solution)/shard_map/ppermute | solution.py:334
  9.1 1.3 collective-permute-start.1
  11.6 3.3 %collective-permute-done.refs_0_.refs_4_ = f32[192,384]{1,0:T(8,128)S(1)} collective-permute-done((f32[192,384]{1,0:T(8,128)}, f32[192,384]{1,0:T(8,128)S(1)}, u32[]{:S(2)}, u32[]{:S(2)}) %collective-permute-start) | collective-permute-done | bytes 294944 | tf_op jit(solution)/shard_map/ppermute | solution.py:334
  14.8 4.0 %collective-permute-done.1.refs_1_.refs_3_ = f32[192,384]{1,0:T(8,128)S(1)} collective-permute-done((f32[192,384]{1,0:T(8,128)}, f32[192,384]{1,0:T(8,128)S(1)}, u32[]{:S(2)}, u32[]{:S(2)}) %collective-permute-start.1) | collective-permute-done | bytes 294944 | tf_op jit(solution)/shard_map/ppermute | solution.py:334
  18.9 1.3 copy-done
  20.2 1.4 give_kernel.2.refs_0_
  21.6 1.3 collective-permute-start.7
  24.5 1.4 keep_kernel.2
  25.8 6.6 %collective-permute-start.8 = (f32[256,384]{1,0:T(8,128)S(1)}, f32[256,384]{1,0:T(8,128)S(1)}, u32[]{:S(2)}, u32[]{:S(2)}) collective-permute-start(f32[256,384]{1,0:T(8,128)S(1)} %get-tuple-element.36.refs_2_), channel_id=1, source_target_pairs={{0,8},{4,12},{24,16},{28,20},{1,9},{5,13},{25,17},{29,21},{2,10},{... | collective-permute-start | bytes 1179656 | tf_op jit(solution)/shard_map/ppermute | solution.py:334
  32.9 1.3 collective-permute-start.10
  36.2 4.7 %collective-permute-done.8.refs_3_ = f32[256,384]{1,0:T(8,128)S(1)} collective-permute-done((f32[256,384]{1,0:T(8,128)S(1)}, f32[256,384]{1,0:T(8,128)S(1)}, u32[]{:S(2)}, u32[]{:S(2)}) %collective-permute-start.8) | collective-permute-done | bytes 393248 | tf_op jit(solution)/shard_map/ppermute | solution.py:334
  41.4 2.0 collective-permute-done.10.refs_5_
  44.6 2.4 %collective-permute-start.15 = (f32[256,384]{1,0:T(8,128)S(1)}, f32[256,384]{1,0:T(8,128)S(1)}, u32[]{:S(2)}, u32[]{:S(2)}) collective-permute-start(f32[256,384]{1,0:T(8,128)S(1)} %get-tuple-element.40.refs_2_), channel_id=1, source_target_pairs={{0,8},{4,12},{24,16},{28,20},{1,9},{5,13},{25,17},{29,21},{2,10},{... | collective-permute-start | bytes 1179656 | tf_op jit(solution)/shard_map/ppermute | solution.py:334
  47.1 1.3 collective-permute-start.18
  49.1 1.9 first_panel.1
  51.0 1.6 collective-permute-start.16
  52.6 1.5 collective-permute-start.17
  54.1 2.4 %collective-permute-done.15.refs_3_ = f32[256,384]{1,0:T(8,128)S(1)} collective-permute-done((f32[256,384]{1,0:T(8,128)S(1)}, f32[256,384]{1,0:T(8,128)S(1)}, u32[]{:S(2)}, u32[]{:S(2)}) %collective-permute-start.15) | collective-permute-done | bytes 393248 | tf_op jit(solution)/shard_map/ppermute | solution.py:334
  58.5 1.6 collective-permute-start.20
  60.8 3.3 %collective-permute-done.18.refs_3_ = f32[256,384]{1,0:T(8,128)S(1)} collective-permute-done((f32[256,384]{1,0:T(8,128)S(1)}, f32[256,384]{1,0:T(8,128)S(1)}, u32[]{:S(2)}, u32[]{:S(2)}) %collective-permute-start.18) | collective-permute-done | bytes 393248 | tf_op jit(solution)/shard_map/ppermute | solution.py:334
  65.9 1.4 stripe_kernel.1
  67.2 1.4 give_kernel.3.refs_0_
  69.4 1.3 collective-permute-start.25
  73.4 7.5 %collective-permute-start.26 = (f32[48,384]{1,0:T(8,128)S(1)}, f32[48,384]{1,0:T(8,128)S(1)}, u32[]{:S(2)}, u32[]{:S(2)}) collective-permute-start(f32[48,384]{1,0:T(8,128)S(1)} %add_kernel.31.refs_0_.refs_2_), channel_id=1, source_target_pairs={{0,8},{4,12},{8,16},{12,20},{16,24},{20,28},{24,0},{28,4},{1,9},{5... | collective-permute-start | bytes 221192 | tf_op jit(solution)/shard_map/ppermute | solution.py:334
  81.0 1.4 keep_kernel.3
  82.4 3.9 %collective-permute-start.31 = (f32[256,384]{1,0:T(8,128)S(1)}, f32[256,384]{1,0:T(8,128)S(1)}, u32[]{:S(2)}, u32[]{:S(2)}) collective-permute-start(f32[256,384]{1,0:T(8,128)S(1)} %get-tuple-element.49.refs_2_), channel_id=1, source_target_pairs={{0,8},{4,12},{24,16},{28,20},{1,9},{5,13},{25,17},{29,21},{2,10},{... | collective-permute-start | bytes 1179656 | tf_op jit(solution)/shard_map/ppermute | solution.py:334
  86.9 1.3 collective-permute-start.32
  88.2 8.5 %collective-permute-start.27 = (f32[48,384]{1,0:T(8,128)S(1)}, f32[48,384]{1,0:T(8,128)S(1)}, u32[]{:S(2)}, u32[]{:S(2)}) collective-permute-start(f32[48,384]{1,0:T(8,128)S(1)} %add_kernel.31.refs_0_.refs_2_), channel_id=1, source_target_pairs={{0,16},{4,20},{8,24},{12,28},{16,0},{20,4},{24,8},{28,12},{1,17},{... | collective-permute-start | bytes 221192 | tf_op jit(solution)/shard_map/ppermute | solution.py:334
  97.7 2.9 %collective-permute-done.27.refs_4_ = f32[48,384]{1,0:T(8,128)S(1)} collective-permute-done((f32[48,384]{1,0:T(8,128)S(1)}, f32[48,384]{1,0:T(8,128)S(1)}, u32[]{:S(2)}, u32[]{:S(2)}) %collective-permute-start.27) | collective-permute-done | bytes 73760 | tf_op jit(solution)/shard_map/ppermute | solution.py:334
  100.7 1.9 collective-permute-done.28.refs_5_
  103.8 1.3 collective-permute-start.36
  105.1 4.6 %collective-permute-start.37 = (f32[256,384]{1,0:T(8,128)S(1)}, f32[256,384]{1,0:T(8,128)S(1)}, u32[]{:S(2)}, u32[]{:S(2)}) collective-permute-start(f32[256,384]{1,0:T(8,128)S(1)} %get-tuple-element.50.refs_2_), channel_id=1, source_target_pairs={{0,8},{4,12},{24,16},{28,20},{1,9},{5,13},{25,17},{29,21},{2,10},{... | collective-permute-start | bytes 1179656 | tf_op jit(solution)/shard_map/ppermute | solution.py:334
  111.6 1.6 collective-permute-start.33
  113.1 1.5 collective-permute-start.34
  116.3 1.9 collective-permute-done.33.refs_3_
  118.2 3.7 %collective-permute-done.34.refs_4_ = f32[96,384]{1,0:T(8,128)S(1)} collective-permute-done((f32[96,384]{1,0:T(8,128)S(1)}, f32[96,384]{1,0:T(8,128)S(1)}, u32[]{:S(2)}, u32[]{:S(2)}) %collective-permute-start.34) | collective-permute-done | bytes 147488 | tf_op jit(solution)/shard_map/ppermute | solution.py:343
  123.7 2.6 %gram_kernel.1 = (f32[192,384]{1,0:T(8,128)S(1)}, f32[192,384]{1,0:T(8,128)S(1)}) custom-call(f32[256,384]{1,0:T(8,128)S(1)} %add_kernel.35.refs_0_.refs_2_, s32[3]{0:T(128)S(1)} %pad_add_fusion.refs_2_.refs_1_, f32[256,384]{1,0:T(8,128)S(1)} %pick_kernel.6.refs_0_.refs_2_.refs_4_, f32[256,384]{1,0:T(8,128)S(1)} %pick_kernel.7.refs_0_.refs_3_.refs_5_, ...), custom_call_target="tpu_custom_call" | custom-call | flops 1 | bytes 1 | tf_op jit(solution)/shard_map/gram_kernel/pallas_call | solution.py:54
  128.1 3.1 %collective-permute-start.43 = (f32[256,384]{1,0:T(8,128)S(1)}, f32[256,384]{1,0:T(8,128)S(1)}, u32[]{:S(2)}, u32[]{:S(2)}) collective-permute-start(f32[256,384]{1,0:T(8,128)S(1)} %get-tuple-element.48.refs_0_.refs_2_), channel_id=1, source_target_pairs={{0,8},{4,12},{24,16},{28,20},{1,9},{5,13},{25,17},{29,21},{2,10},{... | collective-permute-start | bytes 1179656 | tf_op jit(solution)/shard_map/ppermute | solution.py:334
  131.9 1.3 collective-permute-start.44
  133.9 1.7 second_product.1
  136.2 3.1 %collective-permute-done.43.refs_3_ = f32[256,384]{1,0:T(8,128)S(1)} collective-permute-done((f32[256,384]{1,0:T(8,128)S(1)}, f32[256,384]{1,0:T(8,128)S(1)}, u32[]{:S(2)}, u32[]{:S(2)}) %collective-permute-start.43) | collective-permute-done | bytes 393248 | tf_op jit(solution)/shard_map/ppermute | solution.py:334
  140.7 1.6 collective-permute-start.46
  143.4 1.3 collective-permute-start.48
  144.6 2.8 %collective-permute-done.45.refs_3_ = f32[96,384]{1,0:T(8,128)S(1)} collective-permute-done((f32[96,384]{1,0:T(8,128)S(1)}, f32[96,384]{1,0:T(8,128)S(1)}, u32[]{:S(2)}, u32[]{:S(2)}) %collective-permute-start.45) | collective-permute-done | bytes 147488 | tf_op jit(solution)/shard_map/ppermute | solution.py:343
  148.0 1.6 collective-permute-start.49
  150.1 1.3 collective-permute-start.53
  152.0 1.7 collective-permute-done.48.refs_3_
  153.7 1.3 collective-permute-start.54
  156.8 1.3 collective-permute-start.55
  158.1 1.6 collective-permute-done.52.refs_4_
  159.7 15.7 %inverse_kernel.1 = (f32[384,384]{1,0:T(8,128)S(1)}, f32[384,384]{1,0:T(8,128)S(1)}) custom-call(f32[256,384]{1,0:T(8,128)S(1)} %add_kernel.44.refs_0_.refs_2_, s32[3]{0:T(128)S(1)} %pad_add_fusion.refs_2_.refs_1_, f32[384,384]{1,0:T(8,128)S(1)} %gather_kernel.1.refs_0_.refs_2_, f32[192,384]{1,0:T(8,128)S(1)} %add_kernel.42.refs_0_.refs_3_, ...), custom_call_target="tpu_custom_call" | custom-call | flops 1 | bytes 1 | tf_op jit(solution)/shard_map/inverse_kernel/pallas_call | solution.py:54
  177.2 2.2 %collective-permute-done.55.refs_3_ = f32[256,384]{1,0:T(8,128)S(1)} collective-permute-done((f32[256,384]{1,0:T(8,128)S(1)}, f32[256,384]{1,0:T(8,128)S(1)}, u32[]{:S(2)}, u32[]{:S(2)}) %collective-permute-start.55) | collective-permute-done | bytes 393248 | tf_op jit(solution)/shard_map/ppermute | solution.py:334
  180.1 1.5 left_kernel.1
  182.8 2.9 %right_kernel.1 = (f32[1536,384]{1,0:T(8,128)S(1)}, f32[1,384]{1,0:T(1,128)S(1)}) custom-call(f32[1,384]{1,0:T(1,128)S(1)} %get-tuple-element.60.refs_0_.refs_2_, s32[3]{0:T(128)S(1)} %pad_add_fusion.refs_2_.refs_1_, f32[256,384]{1,0:T(8,128)S(1)} %pick_kernel.9.refs_0_.refs_2_, f32[256,384]{1,0:T(8,128)S(1)} %pick_kernel.10.refs_0_.refs_3_, ...), custom_call_target="tpu_custom_call" | custom-call | flops 1 | bytes 1 | tf_op jit(solution)/shard_map/right_kernel/pallas_call | solution.py:54
  185.8 1.4 copy-done.12
  191.3 3.1 %collective-permute-start.63 = (f32[1,384]{1,0:T(1,128)S(1)}, f32[1,384]{1,0:T(1,128)S(1)}, u32[]{:S(2)}, u32[]{:S(2)}) collective-permute-start(f32[1,384]{1,0:T(1,128)S(1)} %add_kernel.45.refs_0_.refs_2_), channel_id=1, source_target_pairs={{0,8},{4,12},{8,16},{12,20},{16,24},{20,28},{24,0},{28,4},{1,9},{5... | collective-permute-start | bytes 4616 | tf_op jit(solution)/shard_map/ppermute | solution.py:334
  199.5 2.9 %carry_two_kernel.1.refs_0_ = f32[192,1536]{1,0:T(8,128)} custom-call(f32[1,384]{1,0:T(1,128)S(1)} %add_kernel.45.refs_0_.refs_2_, s32[3]{0:T(128)S(1)} %pad_add_fusion.refs_2_.refs_1_, f32[192,1536]{1,0:T(8,128)S(1)} %copy-done.1, bf16[192,1536]{1,0:T(8,128)(2,1)S(1)} %copy-done.5, f32[256,384]{1,0:T(8,128)S(1)} %pick_kernel.6.refs_0_.refs_2_.refs_4_, ...), custom_call_target="tpu_custom_call" | custom-call | flops 1 | bytes 1 | tf_op jit(solution)/shard_map/carry_two_kernel/pallas_call | solution.py:54
  202.4 2.8 %collective-permute-start.65 = (f32[1,384]{1,0:T(1,128)S(1)}, f32[1,384]{1,0:T(1,128)S(1)}, u32[]{:S(2)}, u32[]{:S(2)}) collective-permute-start(f32[1,384]{1,0:T(1,128)S(1)} %add_kernel.45.refs_0_.refs_2_), channel_id=1, source_target_pairs={{0,24},{4,28},{8,0},{12,4},{16,8},{20,12},{24,16},{28,20},{1,25},{... | collective-permute-start | bytes 4616 | tf_op jit(solution)/shard_map/ppermute | solution.py:334
  205.3 1.3 copy-done.8
  207.3 3.7 %carry_one_kernel.1.refs_0_ = f32[192,1536]{1,0:T(8,128)} custom-call(f32[1,384]{1,0:T(1,128)S(1)} %total_kernel.4.refs_0_, s32[3]{0:T(128)S(1)} %pad_add_fusion.refs_2_.refs_1_, f32[192,1536]{1,0:T(8,128)S(1)} %copy-done.2, bf16[192,1536]{1,0:T(8,128)(2,1)S(1)} %copy-done.7, f32[96,384]{1,0:T(8,128)S(1)} %copy-done.15, f32[96,384]{1,0:T(8,128)S(1)} %copy-done.11, ...), custom_call_target="tpu_custom_call" | custom-call | flops 1 | bytes 1 | tf_op jit(solution)/shard_map/carry_one_kernel/pallas_call | solution.py:54
  211.1 1.3 copy-done.9
  212.9 1.5 dynamic-slice_multiply_fusion.1
  (181 shorter events, 47.8 us)
Async XLA Ops:
  0.6 10.8 %collective-permute-start.2 = (f32[48,384]{1,0:T(8,128)}, f32[48,384]{1,0:T(8,128)S(1)}, u32[]{:S(2)}, u32[]{:S(2)}) collective-permute-start(f32[48,384]{1,0:T(8,128)} %param.11), channel_id=1, source_target_pairs={{0,1},{1,0},{2,3},{3,2},{4,5},{5,4},{6,7},{7,6},{8,9},{9,8},{10,11... | collective-permute-start | bytes 221192 | tf_op jit(solution)/shard_map/ppermute | solution.py:343
  3.6 7.9 %collective-permute-start.3 = (f32[48,384]{1,0:T(8,128)}, f32[48,384]{1,0:T(8,128)S(1)}, u32[]{:S(2)}, u32[]{:S(2)}) collective-permute-start(f32[48,384]{1,0:T(8,128)} %param.11), channel_id=1, source_target_pairs={{0,2},{1,3},{2,0},{3,1},{4,6},{5,7},{6,4},{7,5},{8,10},{9,11},{10,... | collective-permute-start | bytes 221192 | tf_op jit(solution)/shard_map/ppermute | solution.py:343
  5.2 6.4 %collective-permute-start.4 = (f32[48,384]{1,0:T(8,128)}, f32[48,384]{1,0:T(8,128)S(1)}, u32[]{:S(2)}, u32[]{:S(2)}) collective-permute-start(f32[48,384]{1,0:T(8,128)} %param.11), channel_id=1, source_target_pairs={{0,3},{1,2},{2,1},{3,0},{4,7},{5,6},{6,5},{7,4},{8,11},{9,10},{10,... | collective-permute-start | bytes 221192 | tf_op jit(solution)/shard_map/ppermute | solution.py:343
  5.2 9.7 %collective-permute-start = (f32[192,384]{1,0:T(8,128)}, f32[192,384]{1,0:T(8,128)S(1)}, u32[]{:S(2)}, u32[]{:S(2)}) collective-permute-start(f32[192,384]{1,0:T(8,128)} %refs_4_.3), channel_id=1, source_target_pairs={{0,8},{4,12},{8,16},{12,20},{16,24},{20,28},{1,9},{5,13},{9,17},{1... | collective-permute-start | bytes 884744 | tf_op jit(solution)/shard_map/ppermute | solution.py:334
  9.1 9.7 %collective-permute-start.1 = (f32[192,384]{1,0:T(8,128)}, f32[192,384]{1,0:T(8,128)S(1)}, u32[]{:S(2)}, u32[]{:S(2)}) collective-permute-start(f32[192,384]{1,0:T(8,128)} %refs_4_.3), channel_id=1, source_target_pairs={{8,0},{12,4},{16,8},{20,12},{24,16},{28,20},{9,1},{13,5},{17,9},{2... | collective-permute-start | bytes 884744 | tf_op jit(solution)/shard_map/ppermute | solution.py:334
  21.5 2.9 %collective-permute-start.5 = (f32[768,384]{1,0:T(8,128)S(1)}, f32[768,384]{1,0:T(8,128)S(1)}, u32[]{:S(2)}, u32[]{:S(2)}) collective-permute-start(f32[768,384]{1,0:T(8,128)S(1)} %give_kernel.2.refs_0_), channel_id=1, source_target_pairs={{0,4},{4,0},{8,12},{12,8},{16,20},{20,16},{24,28},{28,24},{1,5},{5... | collective-permute-start | bytes 3538952 | tf_op jit(solution)/shard_map/ppermute | solution.py:330
  21.6 11.3 %collective-permute-start.7 = (f32[192,384]{1,0:T(8,128)S(1)}, f32[192,384]{1,0:T(8,128)S(1)}, u32[]{:S(2)}, u32[]{:S(2)}) collective-permute-start(f32[192,384]{1,0:T(8,128)S(1)} %collective-permute-done.1.refs_1_.refs_3_), channel_id=1, source_target_pairs={{8,0},{12,4},{16,8},{20,12},{9,1},{13,5},{17,9},{21,13},{10,2},{14... | collective-permute-start | bytes 884744 | tf_op jit(solution)/shard_map/ppermute | solution.py:334
  22.9 11.3 %collective-permute-start.6 = (f32[192,384]{1,0:T(8,128)S(1)}, f32[192,384]{1,0:T(8,128)S(1)}, u32[]{:S(2)}, u32[]{:S(2)}) collective-permute-start(f32[192,384]{1,0:T(8,128)S(1)} %collective-permute-done.refs_0_.refs_4_), channel_id=1, source_target_pairs={{8,16},{12,20},{16,24},{20,28},{9,17},{13,21},{17,25},{21,29},{10,... | collective-permute-start | bytes 884744 | tf_op jit(solution)/shard_map/ppermute | solution.py:334
  25.8 15.0 %collective-permute-start.8 = (f32[256,384]{1,0:T(8,128)S(1)}, f32[256,384]{1,0:T(8,128)S(1)}, u32[]{:S(2)}, u32[]{:S(2)}) collective-permute-start(f32[256,384]{1,0:T(8,128)S(1)} %get-tuple-element.36.refs_2_), channel_id=1, source_target_pairs={{0,8},{4,12},{24,16},{28,20},{1,9},{5,13},{25,17},{29,21},{2,10},{... | collective-permute-start | bytes 1179656 | tf_op jit(solution)/shard_map/ppermute | solution.py:334
  32.9 10.5 %collective-permute-start.10 = (f32[192,384]{1,0:T(8,128)S(1)}, f32[192,384]{1,0:T(8,128)S(1)}, u32[]{:S(2)}, u32[]{:S(2)}) collective-permute-start(f32[192,384]{1,0:T(8,128)S(1)} %collective-permute-done.7.refs_3_), channel_id=1, source_target_pairs={{8,0},{12,4},{9,1},{13,5},{10,2},{14,6},{11,3},{15,7}} | collective-permute-start | bytes 884744 | tf_op jit(solution)/shard_map/ppermute | solution.py:334
  34.2 9.2 %collective-permute-start.9 = (f32[192,384]{1,0:T(8,128)S(1)}, f32[192,384]{1,0:T(8,128)S(1)}, u32[]{:S(2)}, u32[]{:S(2)}) collective-permute-start(f32[192,384]{1,0:T(8,128)S(1)} %collective-permute-done.6.refs_2_), channel_id=1, source_target_pairs={{16,24},{20,28},{17,25},{21,29},{18,26},{22,30},{19,27},{23,31}} | collective-permute-start | bytes 884744 | tf_op jit(solution)/shard_map/ppermute | solution.py:334
  34.9 12.1 %collective-permute-start.11 = (f32[192,384]{1,0:T(8,128)S(1)}, f32[192,384]{1,0:T(8,128)S(1)}, u32[]{:S(2)}, u32[]{:S(2)}) collective-permute-start(f32[192,384]{1,0:T(8,128)S(1)} %copy-done.24), channel_id=1, source_target_pairs={{0,4},{4,0},{8,12},{12,8},{16,20},{20,16},{24,28},{28,24},{1,5},{5... | collective-permute-start | bytes 884744 | tf_op jit(solution)/shard_map/ppermute | solution.py:330
  35.6 12.8 %collective-permute-start.13 = (f32[192,384]{1,0:T(8,128)S(1)}, f32[192,384]{1,0:T(8,128)S(1)}, u32[]{:S(2)}, u32[]{:S(2)}) collective-permute-start(f32[192,384]{1,0:T(8,128)S(1)} %add_kernel.23.refs_0_.refs_6_), channel_id=1, source_target_pairs={{0,4},{4,0},{8,12},{12,8},{16,20},{20,16},{24,28},{28,24},{1,5},{5... | collective-permute-start | bytes 884744 | tf_op jit(solution)/shard_map/ppermute | solution.py:330
  44.0 5.1 %collective-permute-start.12 = (f32[192,384]{1,0:T(8,128)S(1)}, f32[192,384]{1,0:T(8,128)S(1)}, u32[]{:S(2)}, u32[]{:S(2)}) collective-permute-start(f32[192,384]{1,0:T(8,128)S(1)} %get-tuple-element.38.refs_5_), channel_id=1, source_target_pairs={{0,4},{4,0},{8,12},{12,8},{16,20},{20,16},{24,28},{28,24},{1,5},{5... | collective-permute-start | bytes 884744 | tf_op jit(solution)/shard_map/ppermute | solution.py:330
  44.1 5.0 %collective-permute-start.14 = (f32[192,384]{1,0:T(8,128)S(1)}, f32[192,384]{1,0:T(8,128)S(1)}, u32[]{:S(2)}, u32[]{:S(2)}) collective-permute-start(f32[192,384]{1,0:T(8,128)S(1)} %get-tuple-element.37.refs_0_.refs_7_), channel_id=1, source_target_pairs={{0,4},{4,0},{8,12},{12,8},{16,20},{20,16},{24,28},{28,24},{1,5},{5... | collective-permute-start | bytes 884744 | tf_op jit(solution)/shard_map/ppermute | solution.py:330
  44.6 11.9 %collective-permute-start.15 = (f32[256,384]{1,0:T(8,128)S(1)}, f32[256,384]{1,0:T(8,128)S(1)}, u32[]{:S(2)}, u32[]{:S(2)}) collective-permute-start(f32[256,384]{1,0:T(8,128)S(1)} %get-tuple-element.40.refs_2_), channel_id=1, source_target_pairs={{0,8},{4,12},{24,16},{28,20},{1,9},{5,13},{25,17},{29,21},{2,10},{... | collective-permute-start | bytes 1179656 | tf_op jit(solution)/shard_map/ppermute | solution.py:334
  47.1 17.0 %collective-permute-start.18 = (f32[256,384]{1,0:T(8,128)S(1)}, f32[256,384]{1,0:T(8,128)S(1)}, u32[]{:S(2)}, u32[]{:S(2)}) collective-permute-start(f32[256,384]{1,0:T(8,128)S(1)} %get-tuple-element.35.refs_0_.refs_2_), channel_id=1, source_target_pairs={{0,8},{4,12},{24,16},{28,20},{1,9},{5,13},{25,17},{29,21},{2,10},{... | collective-permute-start | bytes 1179656 | tf_op jit(solution)/shard_map/ppermute | solution.py:334
  48.4 16.2 %collective-permute-start.19 = (f32[256,384]{1,0:T(8,128)S(1)}, f32[256,384]{1,0:T(8,128)S(1)}, u32[]{:S(2)}, u32[]{:S(2)}) collective-permute-start(f32[256,384]{1,0:T(8,128)S(1)} %add_kernel.24.refs_0_.refs_2_), channel_id=1, source_target_pairs={{8,16},{12,20},{16,8},{20,12},{9,17},{13,21},{17,9},{21,13},{10,18... | collective-permute-start | bytes 1179656 | tf_op jit(solution)/shard_map/ppermute | solution.py:334
  51.0 6.0 %collective-permute-start.16 = (f32[96,384]{1,0:T(8,128)S(1)}, f32[96,384]{1,0:T(8,128)S(1)}, u32[]{:S(2)}, u32[]{:S(2)}) collective-permute-start(f32[96,384]{1,0:T(8,128)S(1)} %get-tuple-element.41.refs_2_), channel_id=1, source_target_pairs={{0,1},{1,0},{2,3},{3,2},{4,5},{5,4},{6,7},{7,6},{8,9},{9,8},{10,11... | collective-permute-start | bytes 442376 | tf_op jit(solution)/shard_map/ppermute | solution.py:343
  52.6 5.3 %collective-permute-start.17 = (f32[96,384]{1,0:T(8,128)S(1)}, f32[96,384]{1,0:T(8,128)S(1)}, u32[]{:S(2)}, u32[]{:S(2)}) collective-permute-start(f32[96,384]{1,0:T(8,128)S(1)} %get-tuple-element.39.refs_0_.refs_4_), channel_id=1, source_target_pairs={{0,2},{1,3},{2,0},{3,1},{4,6},{5,7},{6,4},{7,5},{8,10},{9,11},{10,... | collective-permute-start | bytes 442376 | tf_op jit(solution)/shard_map/ppermute | solution.py:343
  58.5 6.8 %collective-permute-start.20 = (f32[96,384]{1,0:T(8,128)S(1)}, f32[96,384]{1,0:T(8,128)S(1)}, u32[]{:S(2)}, u32[]{:S(2)}) collective-permute-start(f32[96,384]{1,0:T(8,128)S(1)} %get-tuple-element.43.refs_2_), channel_id=1, source_target_pairs={{0,2},{1,3},{2,0},{3,1},{4,6},{5,7},{6,4},{7,5},{8,10},{9,11},{10,... | collective-permute-start | bytes 442376 | tf_op jit(solution)/shard_map/ppermute | solution.py:343
  60.0 5.2 %collective-permute-start.21 = (f32[96,384]{1,0:T(8,128)S(1)}, f32[96,384]{1,0:T(8,128)S(1)}, u32[]{:S(2)}, u32[]{:S(2)}) collective-permute-start(f32[96,384]{1,0:T(8,128)S(1)} %get-tuple-element.42.refs_0_.refs_4_), channel_id=1, source_target_pairs={{0,1},{1,0},{2,3},{3,2},{4,5},{5,4},{6,7},{7,6},{8,9},{9,8},{10,11... | collective-permute-start | bytes 442376 | tf_op jit(solution)/shard_map/ppermute | solution.py:343
  68.6 12.3 %collective-permute-start.23 = (f32[768,384]{1,0:T(8,128)S(1)}, f32[768,384]{1,0:T(8,128)S(1)}, u32[]{:S(2)}, u32[]{:S(2)}) collective-permute-start(f32[768,384]{1,0:T(8,128)S(1)} %give_kernel.3.refs_0_), channel_id=1, source_target_pairs={{0,4},{4,0},{8,12},{12,8},{16,20},{20,16},{24,28},{28,24},{1,5},{5... | collective-permute-start | bytes 3538952 | tf_op jit(solution)/shard_map/ppermute | solution.py:330
  68.7 17.6 %collective-permute-start.24 = (f32[256,384]{1,0:T(8,128)S(1)}, f32[256,384]{1,0:T(8,128)S(1)}, u32[]{:S(2)}, u32[]{:S(2)}) collective-permute-start(f32[256,384]{1,0:T(8,128)S(1)} %add_kernel.26.refs_0_.refs_2_), channel_id=1, source_target_pairs={{8,16},{12,20},{16,8},{20,12},{9,17},{13,21},{17,9},{21,13},{10,18... | collective-permute-start | bytes 1179656 | tf_op jit(solution)/shard_map/ppermute | solution.py:334
  69.4 27.3 %collective-permute-start.25 = (f32[256,384]{1,0:T(8,128)S(1)}, f32[256,384]{1,0:T(8,128)S(1)}, u32[]{:S(2)}, u32[]{:S(2)}) collective-permute-start(f32[256,384]{1,0:T(8,128)S(1)} %add_kernel.29.refs_0_.refs_2_), channel_id=1, source_target_pairs={{8,0},{12,4},{16,24},{20,28},{9,1},{13,5},{17,25},{21,29},{10,2},{... | collective-permute-start | bytes 1179656 | tf_op jit(solution)/shard_map/ppermute | solution.py:334
  70.7 32.5 %collective-permute-start.29 = (f32[256,384]{1,0:T(8,128)S(1)}, f32[256,384]{1,0:T(8,128)S(1)}, u32[]{:S(2)}, u32[]{:S(2)}) collective-permute-start(f32[256,384]{1,0:T(8,128)S(1)} %add_kernel.28.refs_0_.refs_2_), channel_id=1, source_target_pairs={{8,16},{12,20},{16,8},{20,12},{9,17},{13,21},{17,9},{21,13},{10,18... | collective-permute-start | bytes 1179656 | tf_op jit(solution)/shard_map/ppermute | solution.py:334
  73.4 14.8 %collective-permute-start.26 = (f32[48,384]{1,0:T(8,128)S(1)}, f32[48,384]{1,0:T(8,128)S(1)}, u32[]{:S(2)}, u32[]{:S(2)}) collective-permute-start(f32[48,384]{1,0:T(8,128)S(1)} %add_kernel.31.refs_0_.refs_2_), channel_id=1, source_target_pairs={{0,8},{4,12},{8,16},{12,20},{16,24},{20,28},{24,0},{28,4},{1,9},{5... | collective-permute-start | bytes 221192 | tf_op jit(solution)/shard_map/ppermute | solution.py:334
  82.4 30.8 %collective-permute-start.31 = (f32[256,384]{1,0:T(8,128)S(1)}, f32[256,384]{1,0:T(8,128)S(1)}, u32[]{:S(2)}, u32[]{:S(2)}) collective-permute-start(f32[256,384]{1,0:T(8,128)S(1)} %get-tuple-element.49.refs_2_), channel_id=1, source_target_pairs={{0,8},{4,12},{24,16},{28,20},{1,9},{5,13},{25,17},{29,21},{2,10},{... | collective-permute-start | bytes 1179656 | tf_op jit(solution)/shard_map/ppermute | solution.py:334
  86.9 27.7 %collective-permute-start.32 = (f32[256,384]{1,0:T(8,128)S(1)}, f32[256,384]{1,0:T(8,128)S(1)}, u32[]{:S(2)}, u32[]{:S(2)}) collective-permute-start(f32[256,384]{1,0:T(8,128)S(1)} %add_kernel.32.refs_0_.refs_2_), channel_id=1, source_target_pairs={{8,0},{12,4},{16,24},{20,28},{9,1},{13,5},{17,25},{21,29},{10,2},{... | collective-permute-start | bytes 1179656 | tf_op jit(solution)/shard_map/ppermute | solution.py:334
  88.2 12.4 %collective-permute-start.27 = (f32[48,384]{1,0:T(8,128)S(1)}, f32[48,384]{1,0:T(8,128)S(1)}, u32[]{:S(2)}, u32[]{:S(2)}) collective-permute-start(f32[48,384]{1,0:T(8,128)S(1)} %add_kernel.31.refs_0_.refs_2_), channel_id=1, source_target_pairs={{0,16},{4,20},{8,24},{12,28},{16,0},{20,4},{24,8},{28,12},{1,17},{... | collective-permute-start | bytes 221192 | tf_op jit(solution)/shard_map/ppermute | solution.py:334
  96.7 5.9 %collective-permute-start.28 = (f32[48,384]{1,0:T(8,128)S(1)}, f32[48,384]{1,0:T(8,128)S(1)}, u32[]{:S(2)}, u32[]{:S(2)}) collective-permute-start(f32[48,384]{1,0:T(8,128)S(1)} %add_kernel.31.refs_0_.refs_2_), channel_id=1, source_target_pairs={{0,24},{4,28},{8,0},{12,4},{16,8},{20,12},{24,16},{28,20},{1,25},{... | collective-permute-start | bytes 221192 | tf_op jit(solution)/shard_map/ppermute | solution.py:334
  103.8 18.7 %collective-permute-start.36 = (f32[256,384]{1,0:T(8,128)S(1)}, f32[256,384]{1,0:T(8,128)S(1)}, u32[]{:S(2)}, u32[]{:S(2)}) collective-permute-start(f32[256,384]{1,0:T(8,128)S(1)} %add_kernel.33.refs_0_.refs_2_), channel_id=1, source_target_pairs={{8,0},{12,4},{16,24},{20,28},{9,1},{13,5},{17,25},{21,29},{10,2},{... | collective-permute-start | bytes 1179656 | tf_op jit(solution)/shard_map/ppermute | solution.py:334
  105.1 18.0 %collective-permute-start.37 = (f32[256,384]{1,0:T(8,128)S(1)}, f32[256,384]{1,0:T(8,128)S(1)}, u32[]{:S(2)}, u32[]{:S(2)}) collective-permute-start(f32[256,384]{1,0:T(8,128)S(1)} %get-tuple-element.50.refs_2_), channel_id=1, source_target_pairs={{0,8},{4,12},{24,16},{28,20},{1,9},{5,13},{25,17},{29,21},{2,10},{... | collective-permute-start | bytes 1179656 | tf_op jit(solution)/shard_map/ppermute | solution.py:334
  111.6 6.7 %collective-permute-start.33 = (f32[96,384]{1,0:T(8,128)S(1)}, f32[96,384]{1,0:T(8,128)S(1)}, u32[]{:S(2)}, u32[]{:S(2)}) collective-permute-start(f32[96,384]{1,0:T(8,128)S(1)} %order_kernel.1.refs_0_.refs_2_), channel_id=1, source_target_pairs={{0,1},{1,0},{2,3},{3,2},{4,5},{5,4},{6,7},{7,6},{8,9},{9,8},{10,11... | collective-permute-start | bytes 442376 | tf_op jit(solution)/shard_map/ppermute | solution.py:343
  113.1 8.8 %collective-permute-start.34 = (f32[96,384]{1,0:T(8,128)S(1)}, f32[96,384]{1,0:T(8,128)S(1)}, u32[]{:S(2)}, u32[]{:S(2)}) collective-permute-start(f32[96,384]{1,0:T(8,128)S(1)} %order_kernel.1.refs_0_.refs_2_), channel_id=1, source_target_pairs={{0,2},{1,3},{2,0},{3,1},{4,6},{5,7},{6,4},{7,5},{8,10},{9,11},{10,... | collective-permute-start | bytes 442376 | tf_op jit(solution)/shard_map/ppermute | solution.py:343
  114.6 7.3 %collective-permute-start.35 = (f32[96,384]{1,0:T(8,128)S(1)}, f32[96,384]{1,0:T(8,128)S(1)}, u32[]{:S(2)}, u32[]{:S(2)}) collective-permute-start(f32[96,384]{1,0:T(8,128)S(1)} %order_kernel.1.refs_0_.refs_2_), channel_id=1, source_target_pairs={{0,3},{1,2},{2,1},{3,0},{4,7},{5,6},{6,5},{7,4},{8,11},{9,10},{10,... | collective-permute-start | bytes 442376 | tf_op jit(solution)/shard_map/ppermute | solution.py:343
  126.3 1.8 collective-permute-start.38
  126.4 5.4 %collective-permute-start.39 = (f32[256,384]{1,0:T(8,128)S(1)}, f32[256,384]{1,0:T(8,128)S(1)}, u32[]{:S(2)}, u32[]{:S(2)}) collective-permute-start(f32[256,384]{1,0:T(8,128)S(1)} %pick_kernel.6.refs_0_.refs_2_.refs_4_), channel_id=1, source_target_pairs={{0,4},{4,0},{8,12},{12,8},{16,20},{20,16},{24,28},{28,24},{1,5},{5... | collective-permute-start | bytes 1179656 | tf_op jit(solution)/shard_map/ppermute | solution.py:330
  126.9 6.3 %collective-permute-start.41 = (f32[256,384]{1,0:T(8,128)S(1)}, f32[256,384]{1,0:T(8,128)S(1)}, u32[]{:S(2)}, u32[]{:S(2)}) collective-permute-start(f32[256,384]{1,0:T(8,128)S(1)} %pick_kernel.8.refs_0_.refs_4_.refs_6_), channel_id=1, source_target_pairs={{0,4},{4,0},{8,12},{12,8},{16,20},{20,16},{24,28},{28,24},{1,5},{5... | collective-permute-start | bytes 1179656 | tf_op jit(solution)/shard_map/ppermute | solution.py:330
  127.0 6.9 %collective-permute-start.40 = (f32[256,384]{1,0:T(8,128)S(1)}, f32[256,384]{1,0:T(8,128)S(1)}, u32[]{:S(2)}, u32[]{:S(2)}) collective-permute-start(f32[256,384]{1,0:T(8,128)S(1)} %pick_kernel.7.refs_0_.refs_3_.refs_5_), channel_id=1, source_target_pairs={{0,4},{4,0},{8,12},{12,8},{16,20},{20,16},{24,28},{28,24},{1,5},{5... | collective-permute-start | bytes 1179656 | tf_op jit(solution)/shard_map/ppermute | solution.py:330
  127.4 8.2 %collective-permute-start.42 = (f32[256,384]{1,0:T(8,128)S(1)}, f32[256,384]{1,0:T(8,128)S(1)}, u32[]{:S(2)}, u32[]{:S(2)}) collective-permute-start(f32[256,384]{1,0:T(8,128)S(1)} %add_kernel.34.refs_0_.refs_2_), channel_id=1, source_target_pairs={{8,16},{12,20},{16,8},{20,12},{9,17},{13,21},{17,9},{21,13},{10,18... | collective-permute-start | bytes 1179656 | tf_op jit(solution)/shard_map/ppermute | solution.py:334
  128.1 11.3 %collective-permute-start.43 = (f32[256,384]{1,0:T(8,128)S(1)}, f32[256,384]{1,0:T(8,128)S(1)}, u32[]{:S(2)}, u32[]{:S(2)}) collective-permute-start(f32[256,384]{1,0:T(8,128)S(1)} %get-tuple-element.48.refs_0_.refs_2_), channel_id=1, source_target_pairs={{0,8},{4,12},{24,16},{28,20},{1,9},{5,13},{25,17},{29,21},{2,10},{... | collective-permute-start | bytes 1179656 | tf_op jit(solution)/shard_map/ppermute | solution.py:334
  131.9 10.9 %collective-permute-start.44 = (f32[192,384]{1,0:T(8,128)S(1)}, f32[192,384]{1,0:T(8,128)S(1)}, u32[]{:S(2)}, u32[]{:S(2)}) collective-permute-start(f32[192,384]{1,0:T(8,128)S(1)} %add_kernel.36.refs_0_.refs_2_), channel_id=1, source_target_pairs={{0,1},{1,0},{2,3},{3,2},{4,5},{5,4},{6,7},{7,6},{8,9},{9,8},{10,11... | collective-permute-start | bytes 884744 | tf_op jit(solution)/shard_map/ppermute | solution.py:343
  133.2 16.9 %collective-permute-start.47 = (f32[256,384]{1,0:T(8,128)S(1)}, f32[256,384]{1,0:T(8,128)S(1)}, u32[]{:S(2)}, u32[]{:S(2)}) collective-permute-start(f32[256,384]{1,0:T(8,128)S(1)} %add_kernel.35.refs_0_.refs_2_), channel_id=1, source_target_pairs={{8,16},{12,20},{16,8},{20,12},{9,17},{13,21},{17,9},{21,13},{10,18... | collective-permute-start | bytes 1179656 | tf_op jit(solution)/shard_map/ppermute | solution.py:334
  140.0 16.2 %collective-permute-start.51 = (f32[256,384]{1,0:T(8,128)S(1)}, f32[256,384]{1,0:T(8,128)S(1)}, u32[]{:S(2)}, u32[]{:S(2)}) collective-permute-start(f32[256,384]{1,0:T(8,128)S(1)} %add_kernel.38.refs_0_.refs_2_), channel_id=1, source_target_pairs={{8,16},{12,20},{16,8},{20,12},{9,17},{13,21},{17,9},{21,13},{10,18... | collective-permute-start | bytes 1179656 | tf_op jit(solution)/shard_map/ppermute | solution.py:334
  140.7 6.7 %collective-permute-start.46 = (f32[96,384]{1,0:T(8,128)S(1)}, f32[96,384]{1,0:T(8,128)S(1)}, u32[]{:S(2)}, u32[]{:S(2)}) collective-permute-start(f32[96,384]{1,0:T(8,128)S(1)} %get-tuple-element.53.refs_0_.refs_4_), channel_id=1, source_target_pairs={{0,2},{1,3},{2,0},{3,1},{4,6},{5,7},{6,4},{7,5},{8,10},{9,11},{10,... | collective-permute-start | bytes 442376 | tf_op jit(solution)/shard_map/ppermute | solution.py:343
  142.3 5.1 %collective-permute-start.45 = (f32[96,384]{1,0:T(8,128)S(1)}, f32[96,384]{1,0:T(8,128)S(1)}, u32[]{:S(2)}, u32[]{:S(2)}) collective-permute-start(f32[96,384]{1,0:T(8,128)S(1)} %get-tuple-element.54.refs_2_), channel_id=1, source_target_pairs={{0,1},{1,0},{2,3},{3,2},{4,5},{5,4},{6,7},{7,6},{8,9},{9,8},{10,11... | collective-permute-start | bytes 442376 | tf_op jit(solution)/shard_map/ppermute | solution.py:343
  143.4 10.3 %collective-permute-start.48 = (f32[192,384]{1,0:T(8,128)S(1)}, f32[192,384]{1,0:T(8,128)S(1)}, u32[]{:S(2)}, u32[]{:S(2)}) collective-permute-start(f32[192,384]{1,0:T(8,128)S(1)} %add_kernel.39.refs_0_.refs_2_), channel_id=1, source_target_pairs={{0,2},{1,3},{2,0},{3,1},{4,6},{5,7},{6,4},{7,5},{8,10},{9,11},{10,... | collective-permute-start | bytes 884744 | tf_op jit(solution)/shard_map/ppermute | solution.py:343
  148.0 7.6 %collective-permute-start.49 = (f32[96,384]{1,0:T(8,128)S(1)}, f32[96,384]{1,0:T(8,128)S(1)}, u32[]{:S(2)}, u32[]{:S(2)}) collective-permute-start(f32[96,384]{1,0:T(8,128)S(1)} %get-tuple-element.56.refs_2_), channel_id=1, source_target_pairs={{0,2},{1,3},{2,0},{3,1},{4,6},{5,7},{6,4},{7,5},{8,10},{9,11},{10,... | collective-permute-start | bytes 442376 | tf_op jit(solution)/shard_map/ppermute | solution.py:343
  149.6 5.9 %collective-permute-start.50 = (f32[96,384]{1,0:T(8,128)S(1)}, f32[96,384]{1,0:T(8,128)S(1)}, u32[]{:S(2)}, u32[]{:S(2)}) collective-permute-start(f32[96,384]{1,0:T(8,128)S(1)} %get-tuple-element.55.refs_0_.refs_4_), channel_id=1, source_target_pairs={{0,1},{1,0},{2,3},{3,2},{4,5},{5,4},{6,7},{7,6},{8,9},{9,8},{10,11... | collective-permute-start | bytes 442376 | tf_op jit(solution)/shard_map/ppermute | solution.py:343
  150.1 25.3 %collective-permute-start.53 = (f32[256,384]{1,0:T(8,128)S(1)}, f32[256,384]{1,0:T(8,128)S(1)}, u32[]{:S(2)}, u32[]{:S(2)}) collective-permute-start(f32[256,384]{1,0:T(8,128)S(1)} %add_kernel.37.refs_0_.refs_2_), channel_id=1, source_target_pairs={{8,0},{12,4},{16,24},{20,28},{9,1},{13,5},{17,25},{21,29},{10,2},{... | collective-permute-start | bytes 1179656 | tf_op jit(solution)/shard_map/ppermute | solution.py:334
  153.7 22.5 %collective-permute-start.54 = (f32[256,384]{1,0:T(8,128)S(1)}, f32[256,384]{1,0:T(8,128)S(1)}, u32[]{:S(2)}, u32[]{:S(2)}) collective-permute-start(f32[256,384]{1,0:T(8,128)S(1)} %add_kernel.41.refs_0_.refs_2_), channel_id=1, source_target_pairs={{8,0},{12,4},{16,24},{20,28},{9,1},{13,5},{17,25},{21,29},{10,2},{... | collective-permute-start | bytes 1179656 | tf_op jit(solution)/shard_map/ppermute | solution.py:334
  156.8 22.6 %collective-permute-start.55 = (f32[256,384]{1,0:T(8,128)S(1)}, f32[256,384]{1,0:T(8,128)S(1)}, u32[]{:S(2)}, u32[]{:S(2)}) collective-permute-start(f32[256,384]{1,0:T(8,128)S(1)} %add_kernel.44.refs_0_.refs_2_), channel_id=1, source_target_pairs={{8,0},{12,4},{16,24},{20,28},{9,1},{13,5},{17,25},{21,29},{10,2},{... | collective-permute-start | bytes 1179656 | tf_op jit(solution)/shard_map/ppermute | solution.py:334
  158.1 1.6 collective-permute-start.52
  176.0 6.8 %collective-permute-start.56 = (f32[256,384]{1,0:T(8,128)S(1)}, f32[256,384]{1,0:T(8,128)S(1)}, u32[]{:S(2)}, u32[]{:S(2)}) collective-permute-start(f32[256,384]{1,0:T(8,128)S(1)} %pick_kernel.9.refs_0_.refs_2_), channel_id=1, source_target_pairs={{0,4},{4,0},{8,12},{12,8},{16,20},{20,16},{24,28},{28,24},{1,5},{5... | collective-permute-start | bytes 1179656 | tf_op jit(solution)/shard_map/ppermute | solution.py:330
  176.8 6.0 %collective-permute-start.57 = (f32[256,384]{1,0:T(8,128)S(1)}, f32[256,384]{1,0:T(8,128)S(1)}, u32[]{:S(2)}, u32[]{:S(2)}) collective-permute-start(f32[256,384]{1,0:T(8,128)S(1)} %pick_kernel.10.refs_0_.refs_3_), channel_id=1, source_target_pairs={{0,4},{4,0},{8,12},{12,8},{16,20},{20,16},{24,28},{28,24},{1,5},{5... | collective-permute-start | bytes 1179656 | tf_op jit(solution)/shard_map/ppermute | solution.py:330
  180.0 2.8 %collective-permute-start.58 = (f32[256,384]{1,0:T(8,128)S(1)}, f32[256,384]{1,0:T(8,128)S(1)}, u32[]{:S(2)}, u32[]{:S(2)}) collective-permute-start(f32[256,384]{1,0:T(8,128)S(1)} %pick_kernel.11.refs_0_.refs_4_), channel_id=1, source_target_pairs={{0,4},{4,0},{8,12},{12,8},{16,20},{20,16},{24,28},{28,24},{1,5},{5... | collective-permute-start | bytes 1179656 | tf_op jit(solution)/shard_map/ppermute | solution.py:330
  182.3 8.3 %collective-permute-start.59 = (f32[1,384]{1,0:T(1,128)S(1)}, f32[1,384]{1,0:T(1,128)}, u32[]{:S(2)}, u32[]{:S(2)}) collective-permute-start(f32[1,384]{1,0:T(1,128)S(1)} %get-tuple-element.60.refs_0_.refs_2_), channel_id=1, source_target_pairs={{0,4},{4,0},{8,12},{12,8},{16,20},{20,16},{24,28},{28,24},{1,5},{5... | collective-permute-start | bytes 4616 | tf_op jit(solution)/shard_map/ppermute | solution.py:330
  187.2 15.3 %collective-permute-start.60 = (f32[1,384]{1,0:T(1,128)S(1)}, f32[1,384]{1,0:T(1,128)S(1)}, u32[]{:S(2)}, u32[]{:S(2)}) collective-permute-start(f32[1,384]{1,0:T(1,128)S(1)} %get-tuple-element.62.refs_0_.refs_2_), channel_id=1, source_target_pairs={{0,1},{1,0},{2,3},{3,2},{4,5},{5,4},{6,7},{7,6},{8,9},{9,8},{10,11... | collective-permute-start | bytes 4616 | tf_op jit(solution)/shard_map/ppermute | solution.py:343
  188.3 17.0 %collective-permute-start.61 = (f32[1,384]{1,0:T(1,128)S(1)}, f32[1,384]{1,0:T(1,128)}, u32[]{:S(2)}, u32[]{:S(2)}) collective-permute-start(f32[1,384]{1,0:T(1,128)S(1)} %get-tuple-element.62.refs_0_.refs_2_), channel_id=1, source_target_pairs={{0,2},{1,3},{2,0},{3,1},{4,6},{5,7},{6,4},{7,5},{8,10},{9,11},{10,... | collective-permute-start | bytes 4616 | tf_op jit(solution)/shard_map/ppermute | solution.py:343
  189.5 15.8 %collective-permute-start.62 = (f32[1,384]{1,0:T(1,128)S(1)}, f32[1,384]{1,0:T(1,128)}, u32[]{:S(2)}, u32[]{:S(2)}) collective-permute-start(f32[1,384]{1,0:T(1,128)S(1)} %get-tuple-element.62.refs_0_.refs_2_), channel_id=1, source_target_pairs={{0,3},{1,2},{2,1},{3,0},{4,7},{5,6},{6,5},{7,4},{8,11},{9,10},{10,... | collective-permute-start | bytes 4616 | tf_op jit(solution)/shard_map/ppermute | solution.py:343
  191.3 19.7 %collective-permute-start.63 = (f32[1,384]{1,0:T(1,128)S(1)}, f32[1,384]{1,0:T(1,128)S(1)}, u32[]{:S(2)}, u32[]{:S(2)}) collective-permute-start(f32[1,384]{1,0:T(1,128)S(1)} %add_kernel.45.refs_0_.refs_2_), channel_id=1, source_target_pairs={{0,8},{4,12},{8,16},{12,20},{16,24},{20,28},{24,0},{28,4},{1,9},{5... | collective-permute-start | bytes 4616 | tf_op jit(solution)/shard_map/ppermute | solution.py:334
  194.5 16.6 %collective-permute-start.64 = (f32[1,384]{1,0:T(1,128)S(1)}, f32[1,384]{1,0:T(1,128)S(1)}, u32[]{:S(2)}, u32[]{:S(2)}) collective-permute-start(f32[1,384]{1,0:T(1,128)S(1)} %add_kernel.45.refs_0_.refs_2_), channel_id=1, source_target_pairs={{0,16},{4,20},{8,24},{12,28},{16,0},{20,4},{24,8},{28,12},{1,17},{... | collective-permute-start | bytes 4616 | tf_op jit(solution)/shard_map/ppermute | solution.py:334
  202.4 8.6 %collective-permute-start.65 = (f32[1,384]{1,0:T(1,128)S(1)}, f32[1,384]{1,0:T(1,128)S(1)}, u32[]{:S(2)}, u32[]{:S(2)}) collective-permute-start(f32[1,384]{1,0:T(1,128)S(1)} %add_kernel.45.refs_0_.refs_2_), channel_id=1, source_target_pairs={{0,24},{4,28},{8,0},{12,4},{16,8},{20,12},{24,16},{28,20},{1,25},{... | collective-permute-start | bytes 4616 | tf_op jit(solution)/shard_map/ppermute | solution.py:334
  (30 other events, 172.0 us)
